TPU v7x, 512 devices: a whole 4x8x8 slice. The times are simulated.
512 devices in a mesh: batch: 4 (over y_hi), ctx: 128 (over x, z, y_lo, core).
Axes of the slice: x: 4, y: 8 (y_hi: 4, y_lo: 2; y = y_hi * 2 + y_lo), z: 8, core: 2. Of those that a mesh axis runs over, the one named last changes fastest.
Arguments:
- queries: bfloat16 [4, 32768, 1024], P('batch', 'ctx'), may hold values from -6 to 6
- keys: bfloat16 [4, 32768, 1024], P('batch', 'ctx'), may hold values from -6 to 6
- values: bfloat16 [4, 32768, 1024], P('batch', 'ctx'), may hold values from -6 to 6
- gates: bfloat16 [4, 32768, 1024], P('batch', 'ctx'), may hold values from -6 to 6
- cotangent: bfloat16 [4, 32768, 1024], P('batch', 'ctx'), may hold values from -6 to 6
- rel_bias: float32 [8, 32], replicated, may hold values from -2 to 2
- lengths: int32 [4, 16], P('batch'), may hold values from 1 to 8192, 32768 in all within a row
- send_counts: int32 [4, 128, 128], P('batch'), may hold values from 0 to 3, as said below
- block_pattern: int32 [4, 256, 2], P('batch', 'ctx'), may hold values from 0 to 1, as said below
Outputs:
- query_grad: bfloat16 [4, 32768, 1024], P('batch', 'ctx')
- key_grad: bfloat16 [4, 32768, 1024], P('batch', 'ctx')
- value_grad: bfloat16 [4, 32768, 1024], P('batch', 'ctx')
- gate_grad: bfloat16 [4, 32768, 1024], P('batch', 'ctx')
- bias_grad: float32 [8, 32], replicated
Inputs may be any that keep to these rules, and one draw needn't show every extreme that they name: Every loader's row of send_counts[g] and every owner's column sums to 256; every loader hands exactly 3 rows to some owner and every owner receives exactly 3 rows from some loader. `block_pattern`: entry j of a query block's row says whether it attends the block j blocks back; entry 0 is always 1. The 16 lengths of a group sum to 32768; the longest is exactly 8192.
All inputs are finite; a program needn't handle non-finite values.
Results may differ from a plain program's by a relative error of at most 0.0058.
Values may be sent and summed in bfloat16 or wider, within the bound.
A program may use at most 64 MiB of HBM per device.

v0:
```python
import math

import jax
import jax.numpy as jnp
from jax import lax
from jax.sharding import PartitionSpec as P

BLOCK = 128
WIN_BLK = 2


EPS = 1e-05
HIGH = lax.Precision.HIGHEST


def shifted(block, axis, distance):
    devices = range(lax.axis_size(axis))
    route = [(i - distance, i) for i in devices if i - distance in devices]
    return lax.ppermute(block, axis, route)


def segment_of(places, ends):
    return jnp.sum((places[..., None] >= ends).astype(jnp.int32), axis=-1)


def window_mask(starts, flags, ends, key_limit, block, window):
    offsets = jnp.arange(block, dtype=jnp.int32)
    place_q = starts[:, None] + offsets[None, :]
    moves = (jnp.arange(window, dtype=jnp.int32) - (window - 1)) * block
    place_k = starts[:, None, None] + moves[None, :, None] + offsets[None, None, :]
    hist_q = segment_of(place_q, ends)
    hist_k = segment_of(place_k, ends)
    live = (place_k[:, None] <= place_q[:, :, None, None]) & (place_k[:, None] >= 0)
    live = live & (place_k[:, None] < key_limit) & (hist_k[:, None] == hist_q[:, :, None, None])
    return live.astype(jnp.float32) * flags[:, ::-1][:, None, :, None]


def bias_table(rel_bias, block, window):
    buckets = rel_bias.shape[1]
    span = window * block
    grid = (block, window, block)
    row_i = lax.broadcasted_iota(jnp.int32, grid, 0)
    slot_w = lax.broadcasted_iota(jnp.int32, grid, 1)
    col_c = lax.broadcasted_iota(jnp.int32, grid, 2)
    distance = jnp.clip(row_i + (window - 1 - slot_w) * block - col_c, 0, span - 1)
    bucket = (distance * buckets // span).reshape(-1)
    onehot = (jnp.arange(buckets, dtype=jnp.int32)[:, None] == bucket[None, :]).astype(jnp.float32)
    full = jnp.einsum("hk,kp->hp", rel_bias, onehot, precision=HIGH)
    return (full.reshape(rel_bias.shape[0], block, window, block), onehot)


def windows(ext_rows, count, block, window):
    pieces = ext_rows.reshape(-1, block, ext_rows.shape[-1])
    return jnp.stack([pieces[w : w + count] for w in range(window)], axis=1)


def fold_window(terms):
    count, window, block, width = terms.shape
    total = jnp.zeros((count + window - 1, block, width), jnp.float32)
    for w in range(window):
        total = total + jnp.pad(terms[:, w], ((w, window - 1 - w), (0, 0), (0, 0)))
    return total.reshape(-1, width)


def attend_forward(query_blocks, key_win, value_win, mask, bias_full):
    heads = bias_full.shape[0]
    count, block, width = query_blocks.shape
    window = key_win.shape[1]
    size = width // heads
    mask_scaled = mask * (1.0 / (window * block))
    query_heads = query_blocks.reshape(count, block, heads, size)
    key_heads = key_win.reshape(count, window, block, heads, size)
    value_heads = value_win.reshape(count, window, block, heads, size)
    raw = jnp.einsum(
        "nrhd,nwchd->nhrwc", query_heads, key_heads, preferred_element_type=jnp.float32
    )
    scores = raw * size ** (-0.5) + bias_full[None]
    weights = (jax.nn.silu(scores) * mask_scaled[:, None]).astype(jnp.bfloat16)
    output = jnp.einsum(
        "nhrwc,nwchd->nrhd", weights, value_heads, preferred_element_type=jnp.float32
    )
    return (scores, weights, output.reshape(count * block, width))


def attend_backward(query_blocks, key_win, value_win, mask, scores, weights, grad_blocks, heads):
    count, block, width = query_blocks.shape
    window = key_win.shape[1]
    size = width // heads
    mask_scaled = mask * (1.0 / (window * block))
    query_heads = query_blocks.reshape(count, block, heads, size)
    key_heads = key_win.reshape(count, window, block, heads, size)
    value_heads = value_win.reshape(count, window, block, heads, size)
    grad_heads = grad_blocks.reshape(count, block, heads, size)
    grad_weights = jnp.einsum(
        "nrhd,nwchd->nhrwc", grad_heads, value_heads, preferred_element_type=jnp.float32
    )
    gate_sig = jax.nn.sigmoid(scores)
    grad_scores = (
        grad_weights * (gate_sig * (1.0 + scores * (1.0 - gate_sig))) * mask_scaled[:, None]
    )
    grad_low = grad_scores.astype(jnp.bfloat16)
    scale = size ** (-0.5)
    query_grad = (
        jnp.einsum("nhrwc,nwchd->nrhd", grad_low, key_heads, preferred_element_type=jnp.float32)
        * scale
    )
    key_grad = (
        jnp.einsum("nhrwc,nrhd->nwchd", grad_low, query_heads, preferred_element_type=jnp.float32)
        * scale
    )
    value_grad = jnp.einsum(
        "nhrwc,nrhd->nwchd", weights, grad_heads, preferred_element_type=jnp.float32
    )
    return (
        grad_scores,
        query_grad.reshape(count * block, width),
        key_grad.reshape(count, window, block, width),
        value_grad.reshape(count, window, block, width),
    )


def norm_parts(output):
    center = output - jnp.mean(output, axis=-1, keepdims=True)
    inverse = lax.rsqrt(jnp.mean(center * center, axis=-1, keepdims=True) + EPS)
    return (center * inverse, inverse)


def norm_back(grad_normed, normed, inverse):
    return (
        grad_normed
        - jnp.mean(grad_normed, axis=-1, keepdims=True)
        - normed * jnp.mean(grad_normed * normed, axis=-1, keepdims=True)
    ) * inverse


def locate(incl, excl, places, spots):
    source = jnp.sum((incl[:, None] <= places[None, :]).astype(jnp.int32), axis=0)
    picked = jnp.arange(incl.shape[0], dtype=jnp.int32)[:, None] == source[None, :]
    first = jnp.sum(jnp.where(picked, excl[:, None], 0), axis=0)
    return source * spots + places - first


def body(queries, keys, values, gates, cotangent, rel_bias, lengths, send_counts, block_pattern):
    rows = queries.shape[1]
    width = queries.shape[2]
    heads = rel_bias.shape[0]
    block = BLOCK
    window = WIN_BLK
    rim = (window - 1) * block
    blocks_own = rows // block
    peers = lax.axis_size("ctx")
    spots = 3 * rows // (2 * peers)
    where_me = lax.axis_index("ctx")
    table = send_counts[0]
    out_row = lax.dynamic_index_in_dim(table, where_me, 0, keepdims=False)
    in_col = lax.dynamic_index_in_dim(table, where_me, 1, keepdims=False)
    slot_ids = jnp.arange(spots, dtype=jnp.int32)
    places = jnp.arange(rows, dtype=jnp.int32)
    out_start = jnp.cumsum(out_row) - out_row
    in_start = jnp.cumsum(in_col) - in_col
    send_index = jnp.minimum(out_start[:, None] + slot_ids[None, :], rows - 1)
    back_index = jnp.minimum(in_start[:, None] + slot_ids[None, :], rows - 1)
    arrival = locate(in_start + in_col, in_start, places, spots)
    home = locate(out_start + out_row, out_start, places, spots)

    def outgoing(rows_here):
        return jnp.take(rows_here, send_index, axis=0)

    def settle(moved):
        return jnp.take(moved.reshape(-1, width), arrival, axis=0)

    def returning(rows_own):
        return jnp.take(rows_own, back_index, axis=0)

    def landing(moved):
        return jnp.take(moved.reshape(-1, width), home, axis=0)[None]

    moved = (
        lax.all_to_all(outgoing(queries[0]), "ctx", split_axis=0, concat_axis=0, tiled=True),
        lax.all_to_all(outgoing(keys[0]), "ctx", split_axis=0, concat_axis=0, tiled=True),
        lax.all_to_all(outgoing(values[0]), "ctx", split_axis=0, concat_axis=0, tiled=True),
        lax.all_to_all(outgoing(gates[0]), "ctx", split_axis=0, concat_axis=0, tiled=True),
        lax.all_to_all(outgoing(cotangent[0]), "ctx", split_axis=0, concat_axis=0, tiled=True),
    )
    query_own, key_own, value_own, gate_own, cot_own = [settle(item) for item in moved]
    bias_full, onehot = bias_table(rel_bias, block, window)
    tails = shifted((key_own[rows - rim :], value_own[rows - rim :]), "ctx", 1)
    key_ext = jnp.concatenate([tails[0], key_own], axis=0)
    value_ext = jnp.concatenate([tails[1], value_own], axis=0)
    starts = where_me * rows + jnp.arange(blocks_own, dtype=jnp.int32) * block
    flags = block_pattern[0].astype(jnp.float32)
    ends = jnp.cumsum(lengths[0])
    mask = window_mask(starts, flags, ends, rows * peers, block, window)
    key_win = windows(key_ext, blocks_own, block, window)
    value_win = windows(value_ext, blocks_own, block, window)
    query_blocks = query_own.reshape(blocks_own, block, width)
    scores, weights, output = attend_forward(query_blocks, key_win, value_win, mask, bias_full)
    normed, inverse = norm_parts(output)
    gate_grad_own = (cot_own.astype(jnp.float32) * normed).astype(jnp.bfloat16)
    grad_normed = cot_own.astype(jnp.float32) * gate_own.astype(jnp.float32)
    grad_out = norm_back(grad_normed, normed, inverse).astype(jnp.bfloat16)
    grad_scores, query_grad, key_terms, value_terms = attend_backward(
        query_blocks,
        key_win,
        value_win,
        mask,
        scores,
        weights,
        grad_out.reshape(blocks_own, block, width),
        heads,
    )
    key_ext_grad = fold_window(key_terms)
    value_ext_grad = fold_window(value_terms)
    spill = shifted((key_ext_grad[:rim], value_ext_grad[:rim]), "ctx", -1)
    key_rows = key_ext_grad[rim:]
    value_rows = value_ext_grad[rim:]
    key_grad_own = jnp.concatenate(
        [key_rows[: rows - rim], key_rows[rows - rim :] + spill[0]], axis=0
    ).astype(jnp.bfloat16)
    value_grad_own = jnp.concatenate(
        [value_rows[: rows - rim], value_rows[rows - rim :] + spill[1]], axis=0
    ).astype(jnp.bfloat16)
    query_grad_own = query_grad.astype(jnp.bfloat16)
    local_bias = jnp.einsum(
        "hp,kp->hk", grad_scores.sum(0).reshape(heads, -1), onehot, precision=HIGH
    )
    total_bias = lax.psum(local_bias, ("batch", "ctx"))
    bias_grad = total_bias / math.sqrt(lax.axis_size("batch") * peers * rows)
    back = (
        lax.all_to_all(returning(query_grad_own), "ctx", split_axis=0, concat_axis=0, tiled=True),
        lax.all_to_all(returning(key_grad_own), "ctx", split_axis=0, concat_axis=0, tiled=True),
        lax.all_to_all(returning(value_grad_own), "ctx", split_axis=0, concat_axis=0, tiled=True),
        lax.all_to_all(returning(gate_grad_own), "ctx", split_axis=0, concat_axis=0, tiled=True),
    )
    gate_home = landing(back[3])
    return (landing(back[0]), landing(back[1]), landing(back[2]), gate_home, bias_grad)


def solution(mesh):
    return jax.shard_map(
        body,
        mesh=mesh,
        in_specs=(
            P("batch", "ctx", None),
            P("batch", "ctx", None),
            P("batch", "ctx", None),
            P("batch", "ctx", None),
            P("batch", "ctx", None),
            P(),
            P("batch", None),
            P("batch", None, None),
            P("batch", "ctx", None),
        ),
        out_specs=(
            P("batch", "ctx", None),
            P("batch", "ctx", None),
            P("batch", "ctx", None),
            P("batch", "ctx", None),
            P(),
        ),
        check_vma=False,
    )
```

profile of v0, /device:TPU:1, one launch (start us, length us, event | category | flops | bytes accessed | tf_op | source)
XLA Modules:
  0.0 551.0 jit_solution(9016909170260635367)
XLA Ops:
  19.4 4.9 broadcast_select_fusion.7
  24.3 45.7 %all_to_all.45 = bf16[128,3,1024]{2,1,0:T(4,128)(2,1)} all-to-all(bf16[128,3,1024]{2,1,0:T(4,128)(2,1)S(1)} %get-tuple-element.29), channel_id=1, replica_groups=mesh['batch'=4,'ctx'=128] {'ctx'}, dimensions={0} | all-to-all | bytes 1572864 | tf_op jit(solution)/shard_map/all_to_all | solution.py:183
  70.0 36.4 %all_to_all.46 = bf16[128,3,1024]{2,1,0:T(4,128)(2,1)S(1)} all-to-all(bf16[128,3,1024]{2,1,0:T(4,128)(2,1)S(1)} %get-tuple-element.31), channel_id=1, replica_groups=mesh['batch'=4,'ctx'=128] {'ctx'}, dimensions={0} | all-to-all | bytes 1572864 | tf_op jit(solution)/shard_map/all_to_all | solution.py:181
  106.4 7.3 %all-to-all-start.4 = ((bf16[128,3,1024]{2,1,0:T(4,128)(2,1)}), bf16[128,3,1024]{2,1,0:T(4,128)(2,1)S(1)}, u32[]{:S(2)}, u32[]{:S(2)}) async-start(bf16[128,3,1024]{2,1,0:T(4,128)(2,1)} %get-tuple-element.32), calls=%async_computation.4 | async-start | bytes 2097152 | tf_op jit(solution)/shard_map/all_to_all | solution.py:179
  115.1 27.8 %all-to-all-done.4 = bf16[128,3,1024]{2,1,0:T(4,128)(2,1)S(1)} async-done(((bf16[128,3,1024]{2,1,0:T(4,128)(2,1)}), bf16[128,3,1024]{2,1,0:T(4,128)(2,1)S(1)}, u32[]{:S(2)}, u32[]{:S(2)}) %all-to-all-start.4) | async-done | bytes 786464 | tf_op jit(solution)/shard_map/all_to_all | solution.py:179
  142.9 7.9 %all-to-all-start = ((bf16[128,3,1024]{2,1,0:T(4,128)(2,1)}), bf16[128,3,1024]{2,1,0:T(4,128)(2,1)}, u32[]{:S(2)}, u32[]{:S(2)}) async-start(bf16[128,3,1024]{2,1,0:T(4,128)(2,1)} %get-tuple-element.33), calls=%async_computation | async-start | bytes 2097152 | tf_op jit(solution)/shard_map/all_to_all | solution.py:180
  152.7 27.0 %all-to-all-done = bf16[128,3,1024]{2,1,0:T(4,128)(2,1)} async-done(((bf16[128,3,1024]{2,1,0:T(4,128)(2,1)}), bf16[128,3,1024]{2,1,0:T(4,128)(2,1)}, u32[]{:S(2)}, u32[]{:S(2)}) %all-to-all-start) | async-done | bytes 786464 | tf_op jit(solution)/shard_map/all_to_all | solution.py:180
  179.7 7.8 %all-to-all-start.2 = ((bf16[128,3,1024]{2,1,0:T(4,128)(2,1)}), bf16[128,3,1024]{2,1,0:T(4,128)(2,1)}, u32[]{:S(2)}, u32[]{:S(2)}) async-start(bf16[128,3,1024]{2,1,0:T(4,128)(2,1)} %get-tuple-element.30), calls=%async_computation.2 | async-start | bytes 2097152 | tf_op jit(solution)/shard_map/all_to_all | solution.py:182
  202.1 3.9 collective-permute-start
  211.1 8.6 %all-to-all-done.2 = bf16[128,3,1024]{2,1,0:T(4,128)(2,1)} async-done(((bf16[128,3,1024]{2,1,0:T(4,128)(2,1)}), bf16[128,3,1024]{2,1,0:T(4,128)(2,1)}, u32[]{:S(2)}, u32[]{:S(2)}) %all-to-all-start.2) | async-done | bytes 786464 | tf_op jit(solution)/shard_map/all_to_all | solution.py:182
  238.0 3.8 multiply_convert_fusion
  251.2 4.8 fusion.42
  267.4 3.3 reshape.622
  283.0 2.7 gather_fusion.10
  285.7 3.3 reshape.604
  298.1 4.4 broadcast_select_fusion
  302.5 38.8 %all_to_all.47 = bf16[128,3,1024]{2,1,0:T(4,128)(2,1)} all-to-all(bf16[128,3,1024]{2,1,0:T(4,128)(2,1)S(1)} %get-tuple-element.25), channel_id=1, replica_groups=mesh['batch'=4,'ctx'=128] {'ctx'}, dimensions={0} | all-to-all | bytes 1572864 | tf_op jit(solution)/shard_map/all_to_all | solution.py:233
  341.3 36.4 %all_to_all.48 = bf16[128,3,1024]{2,1,0:T(4,128)(2,1)} all-to-all(bf16[128,3,1024]{2,1,0:T(4,128)(2,1)S(1)} %get-tuple-element.26), channel_id=1, replica_groups=mesh['batch'=4,'ctx'=128] {'ctx'}, dimensions={0} | all-to-all | bytes 1572864 | tf_op jit(solution)/shard_map/all_to_all | solution.py:231
  377.7 36.4 %all_to_all.49 = bf16[128,3,1024]{2,1,0:T(4,128)(2,1)S(1)} all-to-all(bf16[128,3,1024]{2,1,0:T(4,128)(2,1)S(1)} %get-tuple-element.27), channel_id=1, replica_groups=mesh['batch'=4,'ctx'=128] {'ctx'}, dimensions={0} | all-to-all | bytes 1572864 | tf_op jit(solution)/shard_map/all_to_all | solution.py:232
  414.1 7.3 %all-to-all-start.5 = ((bf16[128,3,1024]{2,1,0:T(4,128)(2,1)}), bf16[128,3,1024]{2,1,0:T(4,128)(2,1)S(1)}, u32[]{:S(2)}, u32[]{:S(2)}) async-start(bf16[128,3,1024]{2,1,0:T(4,128)(2,1)} %get-tuple-element.28), calls=%async_computation.5 | async-start | bytes 2097152 | tf_op jit(solution)/shard_map/all_to_all | solution.py:230
  421.7 3.0 copy.154
  424.7 3.0 reshape.397
  427.7 3.3 fusion
  431.0 104.8 %psum.7 = f32[8,32]{1,0:T(8,128)S(1)} all-reduce(f32[8,32]{1,0:T(8,128)S(1)} %fusion), channel_id=1, replica_groups=mesh['batch'=4,'ctx'=128] {'batch','ctx'}, use_global_device_ids=true, to_apply=%region_14.17 | all-reduce | flops 256 | bytes 2048 | tf_op jit(solution)/shard_map/psum | solution.py:227
  (207 shorter events, 116.2 us)
Async XLA Ops:
  70.0 43.8 %copy-start.32 = (s32[1,2,2]{2,1,0:T(2,128)S(1)}, s32[1,2,2]{2,1,0:T(2,128)}, u32[]{:S(2)}) copy-start(s32[1,2,2]{2,1,0:T(2,128)} %param.21) | copy-start | bytes 52
  70.0 43.9 %copy-start.33 = (s32[1,16]{1,0:T(1,128)S(1)}, s32[1,16]{1,0:T(1,128)}, u32[]{:S(2)}) copy-start(s32[1,16]{1,0:T(1,128)} %param.19) | copy-start | bytes 196
  70.0 44.1 %copy-start.28 = (s32[1,128,128]{2,1,0:T(8,128)S(1)}, s32[1,128,128]{2,1,0:T(8,128)}, u32[]{:S(2)}) copy-start(s32[1,128,128]{2,1,0:T(8,128)} %param.20) | copy-start | bytes 196612
  106.4 36.5 %all-to-all-start.4 = ((bf16[128,3,1024]{2,1,0:T(4,128)(2,1)}), bf16[128,3,1024]{2,1,0:T(4,128)(2,1)S(1)}, u32[]{:S(2)}, u32[]{:S(2)}) async-start(bf16[128,3,1024]{2,1,0:T(4,128)(2,1)} %get-tuple-element.32), calls=%async_computation.4 | async-start | bytes 2097152 | tf_op jit(solution)/shard_map/all_to_all | solution.py:179
  142.9 45.0 %copy-start.29 = (f32[8,32]{1,0:T(8,128)S(1)}, f32[8,32]{1,0:T(8,128)}, u32[]{:S(2)}) copy-start(f32[8,32]{1,0:T(8,128)} %param.18) | copy-start | bytes 3076
  142.9 36.7 %all-to-all-start = ((bf16[128,3,1024]{2,1,0:T(4,128)(2,1)}), bf16[128,3,1024]{2,1,0:T(4,128)(2,1)}, u32[]{:S(2)}, u32[]{:S(2)}) async-start(bf16[128,3,1024]{2,1,0:T(4,128)(2,1)} %get-tuple-element.33), calls=%async_computation | async-start | bytes 2097152 | tf_op jit(solution)/shard_map/all_to_all | solution.py:180
  179.7 40.0 %all-to-all-start.2 = ((bf16[128,3,1024]{2,1,0:T(4,128)(2,1)}), bf16[128,3,1024]{2,1,0:T(4,128)(2,1)}, u32[]{:S(2)}, u32[]{:S(2)}) async-start(bf16[128,3,1024]{2,1,0:T(4,128)(2,1)} %get-tuple-element.30), calls=%async_computation.2 | async-start | bytes 2097152 | tf_op jit(solution)/shard_map/all_to_all | solution.py:182
  199.1 7.0 %copy-start.34 = (pred[128,3]{0,1:T(4,128)(4,1)S(1)}, pred[128,3]{0,1:T(4,128)(4,1)}, u32[]{:S(2)}) copy-start(pred[128,3]{0,1:T(4,128)(4,1)} %compare_and_fusion.1) | copy-start | bytes 1156
  199.1 7.1 %copy-start.12 = (f32[32768,8]{0,1:T(8,128)S(1)}, f32[32768,8]{0,1:T(8,128)}, u32[]{:S(2)}) copy-start(f32[32768,8]{0,1:T(8,128)} %fusion.1) | copy-start | bytes 3145732
  202.1 31.3 %collective-permute-start = (bf16[128,1024]{1,0:T(8,128)(2,1)}, bf16[128,1024]{1,0:T(8,128)(2,1)S(1)}, u32[]{:S(2)}, u32[]{:S(2)}) collective-permute-start(bf16[128,1024]{1,0:T(8,128)(2,1)} %slice.132), channel_id=1, source_target_pairs={{0,1},{1,2},{2,3},{3,4},{4,5},{5,6},{6,7},{7,8},{8,9},{9,10},{10,1... | collective-permute-start | bytes 786440 | tf_op jit(solution)/shard_map/ppermute | solution.py:19
  211.1 35.2 %copy-start.8 = (bf16[256,1024]{1,0:T(8,128)(2,1)}, bf16[256,1024]{1,0:T(8,128)(2,1)S(1)}, u32[]{:S(2)}) copy-start(bf16[256,1024]{1,0:T(8,128)(2,1)S(1)} %gather_fusion.3) | copy-start | bytes 1572868
  223.3 23.0 %copy-start.9 = (bf16[256,1024]{1,0:T(8,128)(2,1)}, bf16[256,1024]{1,0:T(8,128)(2,1)S(1)}, u32[]{:S(2)}) copy-start(bf16[256,1024]{1,0:T(8,128)(2,1)S(1)} %gather_fusion.5) | copy-start | bytes 1572868
  225.4 9.0 %collective-permute-start.1 = (bf16[128,1024]{1,0:T(8,128)(2,1)}, bf16[128,1024]{1,0:T(8,128)(2,1)S(1)}, u32[]{:S(2)}, u32[]{:S(2)}) collective-permute-start(bf16[128,1024]{1,0:T(8,128)(2,1)} %slice.133), channel_id=1, source_target_pairs={{0,1},{1,2},{2,3},{3,4},{4,5},{5,6},{6,7},{7,8},{8,9},{9,10},{10,1... | collective-permute-start | bytes 786440 | tf_op jit(solution)/shard_map/ppermute | solution.py:19
  229.5 8.5 %copy-start.18 = (bf16[2,128,8,128,1]{1,3,4,2,0:T(8,128)(2,1)}, bf16[2,128,8,128,1]{1,3,4,2,0:T(8,128)(2,1)S(1)}, u32[]{:S(2)}) copy-start(bf16[2,128,8,128,1]{1,3,4,2,0:T(8,128)(2,1)S(1)} %copy.161) | copy-start | bytes 1572868
  234.4 3.6 copy-start.27
  238.0 3.8 copy-start.14
  238.0 3.8 copy-start.23
  238.0 3.8 copy-start.25
  260.0 28.9 %collective-permute-start.3 = (f32[128,1024]{1,0:T(8,128)}, f32[128,1024]{1,0:T(8,128)}, u32[]{:S(2)}, u32[]{:S(2)}) collective-permute-start(f32[128,1024]{1,0:T(8,128)} %get-tuple-element.14), channel_id=1, source_target_pairs={{1,0},{2,1},{3,2},{4,3},{5,4},{6,5},{7,6},{8,7},{9,8},{10,9},{11,1... | collective-permute-start | bytes 1572872 | tf_op jit(solution)/shard_map/ppermute | solution.py:19
  275.9 4.4 copy-start.11
  275.9 4.4 copy-start.15
  278.4 15.2 %collective-permute-start.2 = (f32[128,1024]{1,0:T(8,128)}, f32[128,1024]{1,0:T(8,128)}, u32[]{:S(2)}, u32[]{:S(2)}) collective-permute-start(f32[128,1024]{1,0:T(8,128)} %get-tuple-element.18), channel_id=1, source_target_pairs={{1,0},{2,1},{3,2},{4,3},{5,4},{6,5},{7,6},{8,7},{9,8},{10,9},{11,1... | collective-permute-start | bytes 1572872 | tf_op jit(solution)/shard_map/ppermute | solution.py:19
  377.7 43.8 %copy-start.31 = (s32[128]{0:T(128)S(1)}, s32[128]{0:T(128)}, u32[]{:S(2)}) copy-start(s32[128]{0:T(128)} %copy-done.30) | copy-start | bytes 1540
  414.1 133.0 %all-to-all-start.5 = ((bf16[128,3,1024]{2,1,0:T(4,128)(2,1)}), bf16[128,3,1024]{2,1,0:T(4,128)(2,1)S(1)}, u32[]{:S(2)}, u32[]{:S(2)}) async-start(bf16[128,3,1024]{2,1,0:T(4,128)(2,1)} %get-tuple-element.28), calls=%async_computation.5 | async-start | bytes 2097152 | tf_op jit(solution)/shard_map/all_to_all | solution.py:230
  (19 other events, 34.3 us)
where the time goes:
time: 561 us; the launch traced here: 551 us
  blocking collectives  299 us (53%)
  local copies, waits for them, and re-layouts  101 us (18%)
  waiting for transfers between devices  63.4 us (11%)
  starting transfers between devices  40.7 us (7%)
  other arithmetic  27.4 us (5%)
  matrix products  18.4 us (3%)
    psum x1, blocking collectives, body(): total_bias = lax.psum(local_bias, ('batch', 'ctx'))  105 us
    all_to_all x1, blocking collectives, body(): lax.all_to_all(outgoing(cotangent[0]), 'ctx', split_axis=0, concat_axis=0...  45.7 us
    all_to_all x1, blocking collectives, body(): lax.all_to_all(returning(gate_grad_own), 'ctx', split_axis=0, concat_axis...  38.8 us
    all_to_all x1, blocking collectives, body(): lax.all_to_all(outgoing(values[0]), 'ctx', split_axis=0, concat_axis=0, t...  36.4 us
    all_to_all x1, blocking collectives, body(): lax.all_to_all(returning(value_grad_own), 'ctx', split_axis=0, concat_axi...  36.4 us
    all_to_all x1, blocking collectives, body(): lax.all_to_all(returning(key_grad_own), 'ctx', split_axis=0, concat_axis=...  36.4 us
    all_to_all x1, waiting for transfers between devices, body(): lax.all_to_all(outgoing(queries[0]), 'ctx', split_axis=0, concat_axis=0,...  27.8 us
    all_to_all x1, waiting for transfers between devices, body(): lax.all_to_all(outgoing(keys[0]), 'ctx', split_axis=0, concat_axis=0, til...  27 us
  transfers between devices with their start and end apart: 8, of which 3 were waited for; matrix products, arithmetic and copies ran while one was open for 15% of the time, Pallas kernels for 0%

commit v1 on v0

v1 whole, which is shorter than its diff:
```python
import math

import jax
import jax.numpy as jnp
from jax import lax
from jax.experimental import pallas as pl
from jax.experimental.pallas import tpu as pltpu
from jax.sharding import PartitionSpec as P

MESH = pl.DeviceIdType.MESH
F32 = jnp.float32
BF16 = jnp.bfloat16

NX, NZ, NY, NC = 4, 8, 2, 2
PEERS = NX * NZ * NY * NC
BATCH = 4
ROWS = 256
WIDTH = 1024
HEADS = 8
SIZE = 128
CHUNKS = WIDTH // 128
BLOCK = 128
SPAN = 256
BUCKETS = 32
SLOTS = 3
EPS = 1e-05
SCALE = SIZE ** (-0.5)


def coords(me):
    return me // (NZ * NY * NC), (me // (NY * NC)) % NZ, (me // NC) % NY, me % NC


def place(x, z, y, c):
    return ((x * NZ + z) * NY + y) * NC + c


def partner(me, k, sign=1):
    x, z, y, c = coords(me)
    dx, dz, dy, dc = coords(k)
    if sign < 0:
        dx, dz = NX - dx, NZ - dz
    return place((x + dx) % NX, (z + dz) % NZ, (y + dy) % NY, (c + dc) % NC)


def stage(dst, pick, value_of):
    for c in range(CHUNKS):
        rows = matmul(pick, value_of(slice(c * 128, (c + 1) * 128)), 1, 0)
        dst[pl.ds(c, PEERS * SLOTS, stride=CHUNKS), :] = rows


def unstage(src, pick, write):
    for c in range(CHUNKS):
        rows = src[pl.ds(c, PEERS * SLOTS, stride=CHUNKS), :].astype(BF16)
        write(slice(c * 128, (c + 1) * 128), matmul(pick, rows, 1, 0))


def pack(dst, at, first, second):
    for s in range(SLOTS):
        off = pl.multiple_of((at * SLOTS + s) * CHUNKS, CHUNKS)
        tile = jnp.concatenate([first[pl.ds(off, CHUNKS), :], second[pl.ds(off, CHUNKS), :]], axis=0)
        dst[at * SLOTS + s] = tile.astype(BF16)


def unpack(recv, first, second):
    step = 8

    def some(i, carry):
        for j in range(step):
            p = i * step + j
            tile = recv[p].astype(F32)
            off = pl.multiple_of(p * CHUNKS, CHUNKS)
            first[pl.ds(off, CHUNKS), :] = tile[:CHUNKS]
            second[pl.ds(off, CHUNKS), :] = tile[CHUNKS:]
        return carry

    lax.fori_loop(0, PEERS * SLOTS // step, some, 0)


def ones_where(index, axis):
    shape = (ROWS, PEERS * SLOTS) if axis == 0 else (PEERS * SLOTS, ROWS)
    return jnp.where(lax.broadcasted_iota(jnp.int32, shape, axis) == index, 1.0, 0.0).astype(BF16)


def wait_bytes(ref, sem):
    pltpu.make_async_copy(ref, ref, sem).wait()


def matmul(a, b, ca, cb):
    return lax.dot_general(a, b, (((ca,), (cb,)), ((), ())), preferred_element_type=F32)


def kernel(
    q_in, k_in, v_in, g_in, c_in, rel, lengths, pattern, out_col, out_row, in_col, in_row,
    gq_out, gk_out, gv_out, gg_out, bias_out,
    send, recv_0, recv_1, recv_2, recv_3, stage_a, stage_b, q_own, k_ext, v_ext, gn_own, a_all, d_all, table, mask,
    o_all, go_all, gq_acc, gk_acc, gv_acc, halo_out, halo_in, gs_sum, part, red, cur,
    send_sem, recv_sem, halo_send, halo_recv, red_send, red_recv,
):
    recv = (recv_0, recv_1, recv_2, recv_3)
    me = lax.axis_index("ctx")
    grp = lax.axis_index("batch")
    x, z, y, c = coords(me)

    def ctx(i):
        return {"device_id": (grp, i), "device_id_type": MESH}

    barrier = pltpu.get_barrier_semaphore()

    def greet(k, carry):
        pl.semaphore_signal(barrier, inc=1, **ctx(partner(me, k)))
        return carry

    lax.fori_loop(1, PEERS, greet, 0)
    for d in range(1, BATCH):
        pl.semaphore_signal(barrier, inc=1, device_id=((grp + d) % BATCH, me), device_id_type=MESH)

    def exchange(group, first, second):
        out, into = send.at[group], recv[group]

        def one(k, carry):
            to = partner(me, k)
            pack(out, k, first, second)
            pltpu.make_async_remote_copy(
                src_ref=out.at[pl.ds(k * SLOTS, SLOTS)],
                dst_ref=into.at[pl.ds(k * SLOTS, SLOTS)],
                send_sem=send_sem.at[group],
                recv_sem=recv_sem.at[group],
                **ctx(to),
            ).start()
            return carry

        lax.fori_loop(1, PEERS, one, 0)
        pack(into, 0, first, second)

    def arrived(group):
        wait_bytes(recv[group].at[pl.ds(SLOTS, (PEERS - 1) * SLOTS)], recv_sem.at[group])

    def halo_copy(i, src, dst, to):
        return pltpu.make_async_remote_copy(
            src_ref=src, dst_ref=dst, send_sem=halo_send.at[i], recv_sem=halo_recv.at[i], **ctx(to)
        )

    pick = ones_where(out_col[...], 1)
    stage(stage_a, pick, lambda f: q_in[:, f])
    stage(stage_b, pick, lambda f: k_in[:, f])
    pl.semaphore_wait(barrier, PEERS - 1 + BATCH - 1)
    exchange(0, stage_a, stage_b)
    stage(stage_a, pick, lambda f: v_in[:, f])
    stage(stage_b, pick, lambda f: (c_in[:, f].astype(F32) * g_in[:, f].astype(F32)).astype(BF16))
    exchange(1, stage_a, stage_b)

    row_i = lax.broadcasted_iota(jnp.int32, (BLOCK, SPAN), 0)
    col_c = lax.broadcasted_iota(jnp.int32, (BLOCK, SPAN), 1)
    bucket = (row_i + BLOCK - col_c) >> 3

    def bias_of(h, carry):
        full = jnp.zeros((BLOCK, SPAN), F32)
        for k in range(BUCKETS):
            full = jnp.where(bucket == k, rel[h, k], full)
        table[h] = full
        return carry

    lax.fori_loop(0, HEADS, bias_of, 0)
    for b in range(2):
        pos_q = me * ROWS + b * BLOCK + row_i
        pos_k = me * ROWS + (b - 1) * BLOCK + col_c
        hist_q = jnp.zeros((BLOCK, SPAN), jnp.int32)
        hist_k = jnp.zeros((BLOCK, SPAN), jnp.int32)
        end = jnp.int32(0)
        for i in range(lengths.shape[0]):
            end = end + lengths[i]
            hist_q = hist_q + (pos_q >= end).astype(jnp.int32)
            hist_k = hist_k + (pos_k >= end).astype(jnp.int32)
        flag = jnp.where(col_c >= BLOCK, pattern[2 * b], pattern[2 * b + 1])
        live = (pos_k <= pos_q) & (pos_k >= 0) & (hist_q == hist_k) & (flag > 0)
        mask[b] = jnp.where(live, 1.0 / SPAN, 0.0).astype(F32)

    arrived(0)
    settle = ones_where(in_row[...], 0)
    unpack(recv[0], stage_a, stage_b)

    def put_q(f, v):
        q_own[:, f] = v.astype(BF16)

    def put_k(f, v):
        k_ext[BLOCK:, f] = v.astype(BF16)

    def put_v(f, v):
        v_ext[BLOCK:, f] = v.astype(BF16)

    def put_gn(f, v):
        gn_own[:, f] = v

    after, before = (me + 1) % PEERS, (me + PEERS - 1) % PEERS
    unstage(stage_b, settle, put_k)
    k_halo = halo_copy(0, k_ext.at[pl.ds(ROWS, BLOCK)], k_ext.at[pl.ds(0, BLOCK)], after)
    k_halo.start()
    unstage(stage_a, settle, put_q)

    def score(b):
        def one(h, carry):
            f = pl.ds(pl.multiple_of(h * SIZE, SIZE), SIZE)
            raw = matmul(q_own[pl.ds(b * BLOCK, BLOCK), f], k_ext[pl.ds(b * BLOCK, SPAN), f], 1, 1)
            s = raw * SCALE + table[h]
            sig = jax.nn.sigmoid(s)
            m = mask[b]
            a_all[b, h] = (s * sig * m).astype(BF16)
            d_all[b, h] = sig * (1.0 + s * (1.0 - sig)) * m
            return carry

        lax.fori_loop(0, HEADS, one, 0)

    score(1)
    k_halo.wait_recv()
    score(0)

    arrived(1)
    unpack(recv[1], stage_a, stage_b)
    unstage(stage_a, settle, put_v)
    v_halo = halo_copy(1, v_ext.at[pl.ds(ROWS, BLOCK)], v_ext.at[pl.ds(0, BLOCK)], after)
    v_halo.start()
    unstage(stage_b, settle, put_gn)

    def output(b):
        def one(h, carry):
            f = pl.ds(pl.multiple_of(h * SIZE, SIZE), SIZE)
            o_all[pl.ds(b * BLOCK, BLOCK), f] = matmul(a_all[b, h], v_ext[pl.ds(b * BLOCK, SPAN), f], 1, 0)
            return carry

        lax.fori_loop(0, HEADS, one, 0)

    output(1)
    v_halo.wait_recv()
    output(0)

    def norm(i, carry):
        rows = pl.ds(pl.multiple_of(i * 32, 32), 32)
        out = o_all[rows, :]
        center = out - jnp.mean(out, axis=-1, keepdims=True)
        inverse = lax.rsqrt(jnp.mean(center * center, axis=-1, keepdims=True) + EPS)
        normed = center * inverse
        gn = gn_own[rows, :]
        go = (
            gn
            - jnp.mean(gn, axis=-1, keepdims=True)
            - normed * jnp.mean(gn * normed, axis=-1, keepdims=True)
        ) * inverse
        o_all[rows, :] = normed
        go_all[rows, :] = go.astype(BF16)
        return carry

    lax.fori_loop(0, ROWS // 32, norm, 0)

    def back(b):
        def one(h, carry):
            f = pl.ds(pl.multiple_of(h * SIZE, SIZE), SIZE)
            own = pl.ds(b * BLOCK, BLOCK)
            win = pl.ds(b * BLOCK, SPAN)
            go = go_all[own, f]
            gs = matmul(go, v_ext[win, f], 1, 1) * d_all[b, h]
            low = gs.astype(BF16)
            gq_acc[own, f] = matmul(low, k_ext[win, f], 1, 0) * SCALE
            gk = matmul(low, q_own[own, f], 0, 0) * SCALE
            gv = matmul(a_all[b, h], go, 0, 0)
            if b == 0:
                gs_sum[h] = gs
                halo_out[0, :, f] = gk[:BLOCK].astype(BF16)
                halo_out[1, :, f] = gv[:BLOCK].astype(BF16)
                gk_acc[pl.ds(0, BLOCK), f] = gk[BLOCK:]
                gv_acc[pl.ds(0, BLOCK), f] = gv[BLOCK:]
            else:
                gs_sum[h] += gs
                gk_acc[pl.ds(0, BLOCK), f] += gk[:BLOCK]
                gv_acc[pl.ds(0, BLOCK), f] += gv[:BLOCK]
                gk_acc[pl.ds(BLOCK, BLOCK), f] = gk[BLOCK:]
                gv_acc[pl.ds(BLOCK, BLOCK), f] = gv[BLOCK:]
            return carry

        lax.fori_loop(0, HEADS, one, 0)

    back(0)
    g_halo = halo_copy(2, halo_out, halo_in, before)
    g_halo.start()
    back(1)

    pick = ones_where(in_col[...], 1)
    stage(stage_a, pick, lambda f: o_all[:, f].astype(BF16))
    stage(stage_b, pick, lambda f: gq_acc[:, f].astype(BF16))
    exchange(2, stage_a, stage_b)

    def buckets_of(h, carry):
        gs = gs_sum[h]
        for k in range(BUCKETS):
            picked = jnp.where(bucket == k, gs, 0.0)
            part[pl.ds(h * BUCKETS + k, 1), :] = jnp.sum(picked, axis=0, keepdims=True)
        return carry

    lax.fori_loop(0, HEADS, buckets_of, 0)
    sums = jnp.sum(part[...], axis=1, keepdims=True)
    eye = lax.broadcasted_iota(jnp.int32, (128, 128), 0) == lax.broadcasted_iota(jnp.int32, (128, 128), 1)
    lines = [
        jnp.sum(jnp.where(eye, sums[r * 128 : (r + 1) * 128], 0.0), axis=0, keepdims=True) for r in range(2)
    ]
    first_total = jnp.concatenate(lines + [jnp.zeros((6, 128), F32)], axis=0)

    rounds = (
        (NY * NC, y * NC + c, lambda i: (grp, place(x, z, i // NC, i % NC))),
        (NZ, z, lambda i: (grp, place(x, i, y, c))),
        (NX, x, lambda i: (grp, place(i, z, y, c))),
        (BATCH, grp, lambda i: (i, me)),
    )

    def round_start(r, value):
        n, mine, device = rounds[r]
        cur[r] = value
        red[r, mine] = value
        for d in range(1, n):
            pltpu.make_async_remote_copy(
                src_ref=cur.at[r],
                dst_ref=red.at[r, mine],
                send_sem=red_send.at[r],
                recv_sem=red_recv.at[r],
                device_id=device((mine + d) % n),
                device_id_type=MESH,
            ).start()

    def round_end(r):
        n = rounds[r][0]
        wait_bytes(red.at[r, pl.ds(0, n - 1)], red_recv.at[r])
        total = red[r, 0]
        for i in range(1, n):
            total = total + red[r, i]
        return total

    round_start(0, first_total)

    g_halo.wait_recv()
    for acc, i in ((gk_acc, 0), (gv_acc, 1)):
        acc[BLOCK:, :] = acc[BLOCK:, :] + halo_in[i].astype(F32)
    stage(stage_a, pick, lambda f: gk_acc[:, f].astype(BF16))
    stage(stage_b, pick, lambda f: gv_acc[:, f].astype(BF16))
    exchange(3, stage_a, stage_b)

    round_start(1, round_end(0))
    round_start(2, round_end(1))
    arrived(2)
    land = ones_where(out_row[...], 0)
    unpack(recv[2], stage_a, stage_b)

    def put_gate(f, v):
        gg_out[:, f] = (c_in[:, f].astype(F32) * v).astype(BF16)

    def put_gq(f, v):
        gq_out[:, f] = v.astype(BF16)

    def put_gk(f, v):
        gk_out[:, f] = v.astype(BF16)

    def put_gv(f, v):
        gv_out[:, f] = v.astype(BF16)

    unstage(stage_a, land, put_gate)
    unstage(stage_b, land, put_gq)
    round_start(3, round_end(2))
    bias_out[...] = round_end(3) * (1.0 / math.sqrt(BATCH * PEERS * ROWS))

    arrived(3)
    unpack(recv[3], stage_a, stage_b)
    unstage(stage_a, land, put_gk)
    unstage(stage_b, land, put_gv)

    for group in range(4):
        wait_bytes(send.at[group, pl.ds(SLOTS, (PEERS - 1) * SLOTS)], send_sem.at[group])
    k_halo.wait_send()
    v_halo.wait_send()
    g_halo.wait_send()
    for r in range(4):
        wait_bytes(red.at[r, pl.ds(0, rounds[r][0] - 1)], red_send.at[r])


def slots_of(counts, me):
    ids = jnp.arange(PEERS, dtype=jnp.int32)
    first = jnp.sum(jnp.where(ids[None, :] < ids[:, None], counts[None, :], 0), axis=1)
    slot = jnp.arange(SLOTS, dtype=jnp.int32)

    def ordered(sign):
        other = partner(me, ids, sign)[:, None] == ids[None, :]
        start = jnp.sum(jnp.where(other, first[None, :], 0), axis=1)
        count = jnp.sum(jnp.where(other, counts[None, :], 0), axis=1)
        rows = jnp.where(slot[None, :] < count[:, None], start[:, None] + slot[None, :], -1)
        return rows.reshape(-1)

    return ordered(1)[:, None], ordered(-1)[None, :]


def body(queries, keys, values, gates, cotangent, rel_bias, lengths, send_counts, block_pattern):
    me = lax.axis_index("ctx")
    counts = send_counts[0]
    out_col, out_row = slots_of(lax.dynamic_index_in_dim(counts, me, 0, keepdims=False), me)
    in_col, in_row = slots_of(lax.dynamic_index_in_dim(counts, me, 1, keepdims=False), me)
    vmem = pl.BlockSpec(memory_space=pltpu.VMEM)
    smem = pl.BlockSpec(memory_space=pltpu.SMEM)
    event = jax.ShapeDtypeStruct((ROWS, WIDTH), BF16)
    buffer = (PEERS * SLOTS, 16, 128)
    gq, gk, gv, gg, bias = pl.pallas_call(
        kernel,
        out_shape=(event, event, event, event, jax.ShapeDtypeStruct((8, 128), F32)),
        in_specs=[vmem] * 5 + [smem] * 3 + [vmem] * 4,
        out_specs=(vmem,) * 5,
        scratch_shapes=[
            pltpu.VMEM((4,) + buffer, BF16),
            pltpu.VMEM(buffer, BF16),
            pltpu.VMEM(buffer, BF16),
            pltpu.VMEM(buffer, BF16),
            pltpu.VMEM(buffer, BF16),
            pltpu.VMEM((PEERS * SLOTS * CHUNKS, 128), F32),
            pltpu.VMEM((PEERS * SLOTS * CHUNKS, 128), F32),
            pltpu.VMEM((ROWS, WIDTH), BF16),
            pltpu.VMEM((ROWS + BLOCK, WIDTH), BF16),
            pltpu.VMEM((ROWS + BLOCK, WIDTH), BF16),
            pltpu.VMEM((ROWS, WIDTH), F32),
            pltpu.VMEM((2, HEADS, BLOCK, SPAN), BF16),
            pltpu.VMEM((2, HEADS, BLOCK, SPAN), F32),
            pltpu.VMEM((HEADS, BLOCK, SPAN), F32),
            pltpu.VMEM((2, BLOCK, SPAN), F32),
            pltpu.VMEM((ROWS, WIDTH), F32),
            pltpu.VMEM((ROWS, WIDTH), BF16),
            pltpu.VMEM((ROWS, WIDTH), F32),
            pltpu.VMEM((ROWS, WIDTH), F32),
            pltpu.VMEM((ROWS, WIDTH), F32),
            pltpu.VMEM((2, BLOCK, WIDTH), BF16),
            pltpu.VMEM((2, BLOCK, WIDTH), BF16),
            pltpu.VMEM((HEADS, BLOCK, SPAN), F32),
            pltpu.VMEM((HEADS * BUCKETS, SPAN), F32),
            pltpu.VMEM((4, 8, 8, 128), F32),
            pltpu.VMEM((4, 8, 128), F32),
            pltpu.SemaphoreType.DMA((4,)),
            pltpu.SemaphoreType.DMA((4,)),
            pltpu.SemaphoreType.DMA((3,)),
            pltpu.SemaphoreType.DMA((3,)),
            pltpu.SemaphoreType.DMA((4,)),
            pltpu.SemaphoreType.DMA((4,)),
        ],
        compiler_params=pltpu.CompilerParams(
            collective_id=0, has_side_effects=True, vmem_limit_bytes=56 * 1024 * 1024
        ),
    )(
        queries[0], keys[0], values[0], gates[0], cotangent[0],
        rel_bias, lengths[0], block_pattern[0].reshape(-1),
        out_col, out_row, in_col, in_row,
    )
    return gq[None], gk[None], gv[None], gg[None], bias[:2].reshape(HEADS, BUCKETS)


def solution(mesh):
    event = P("batch", "ctx", None)
    return jax.shard_map(
        body,
        mesh=mesh,
        in_specs=(event,) * 5 + (P(), P("batch", None), P("batch", None, None), event),
        out_specs=(event,) * 4 + (P(),),
        check_vma=False,
    )
```

time: 561 us -> 209 us (0.37)
  the two profiles are of different devices: /device:TPU:1 before, /device:TPU:8 now
where the time goes in v1:
time: 209 us; the launch traced here: 208 us
  Pallas kernels  195 us (93%)
  local copies, waits for them, and re-layouts  11.8 us (6%)
    pallas_call x1, Pallas kernels, body(): pl.pallas_call(kernel, out_shape=(event, event, event, event, jax.ShapeDt...  195 us
    unnamed x14, local copies, waits for them, and re-layouts  6.59 us

profile of v1, /device:TPU:8, one launch (start us, length us, event | category | flops | bytes accessed | tf_op | source)
XLA Modules:
  0.0 208.1 jit_solution(6413585201539115063)
XLA Ops:
  0.6 0.0 copy-start
  0.7 0.7 copy-done
  1.5 0.2 dynamic-slice_reduce_fusion
  1.7 0.7 copy-done.4
  2.3 0.6 reshape_squeeze.3.pattern
  2.9 0.1 select_reduce_fusion.3
  3.0 0.3 select_reduce_fusion.1
  3.3 0.1 add_select_fusion
  3.4 0.8 select_n.352.in_row
  4.2 0.1 add_select_fusion.1
  4.3 0.1 add_select_fusion.3
  4.4 0.1 add_select_fusion.2
  4.5 0.8 select_n.343.out_row
  5.3 0.8 select_n.353.out_col
  6.1 0.8 select_n.354.in_col
  6.9 194.7 %shard_map.128 = (bf16[256,1024]{1,0:T(8,128)(2,1)}, bf16[256,1024]{1,0:T(8,128)(2,1)}, bf16[256,1024]{1,0:T(8,128)(2,1)}, bf16[256,1024]{1,0:T(8,128)(2,1)}, f32[8,128]{1,0:T(8,128)}) custom-call(bf16[256,1024]{1,0:T(8,128)(2,1)} %bitcast.16, bf16[256,1024]{1,0:T(8,128)(2,1)} %bitcast.17, bf16[256,1024]{1,0:T(8,128)(2,1)} %bitcast.18, ...), custom_call_target="tpu_custom_call" | custom-call | tf_op jit(solution)/shard_map/pallas_call | solution.py:406
  201.6 0.7 slice.3
  202.3 0.7 reshape.371
  202.9 1.9 copy.22
  204.9 0.8 copy.23
  205.7 0.4 copy-done.2
  206.1 0.8 copy.24
  206.9 0.4 copy-done.1
  207.3 0.8 copy.25
  (7 shorter events, 0.0 us)
Async XLA Ops:
  0.6 0.8 copy-start
  1.7 0.7 copy-start.4
  202.9 1.9 copy-start.3
  204.9 1.2 copy-start.2
  206.1 1.2 copy-start.1

commit v2 on v1

v2 whole, which is shorter than its diff:
```python
import math

import jax
import jax.numpy as jnp
from jax import lax
from jax.experimental import pallas as pl
from jax.experimental.pallas import tpu as pltpu
from jax.sharding import PartitionSpec as P

MESH = pl.DeviceIdType.MESH
F32 = jnp.float32
BF16 = jnp.bfloat16

NX, NZ, NY, NC = 4, 8, 2, 2
PEERS = NX * NZ * NY * NC
BATCH = 4
ROWS = 256
WIDTH = 1024
HEADS = 8
SIZE = 128
CHUNKS = WIDTH // 128
BLOCK = 128
SPAN = 256
BUCKETS = 32
SLOTS = 3
EPS = 1e-05
LINES = PEERS * SLOTS
STEP = 16
SCALE = SIZE ** (-0.5)


def coords(me):
    return me // (NZ * NY * NC), (me // (NY * NC)) % NZ, (me // NC) % NY, me % NC


def place(x, z, y, c):
    return ((x * NZ + z) * NY + y) * NC + c


def partner(me, k):
    x, z, y, c = coords(me)
    dx, dz, dy, dc = coords(k)
    return place((x + dx) % NX, (z + dz) % NZ, (y + dy) % NY, (c + dc) % NC)


def partners_of(me, k, sign):
    x, z, y, c = coords(me)
    dx, dz, dy, dc = k >> 5, (k >> 2) & 7, (k >> 1) & 1, k & 1
    return place((x + sign * dx) & 3, (z + sign * dz) & 7, (y + dy) & 1, (c + dc) & 1)


def eye_turn(vector):
    eye = lax.broadcasted_iota(jnp.int32, (128, 128), 0) == lax.broadcasted_iota(jnp.int32, (128, 128), 1)
    return jnp.sum(jnp.where(eye, vector, 0.0), axis=1 if vector.shape[0] == 1 else 0, keepdims=True)


def travel(me, row, col, axis, sign):
    shape = (LINES, 128) if axis == 0 else (128, LINES)
    device = lax.broadcasted_iota(jnp.int32, shape, 1 - axis)
    along = lax.broadcasted_iota(jnp.int32, shape, axis)
    k = (along * 171) >> 9
    same = partners_of(me, k, sign) == device
    pairs = (128, 128)
    below = lax.broadcasted_iota(jnp.int32, pairs, 1 - axis) < lax.broadcasted_iota(jnp.int32, pairs, axis)
    counts = row if axis == 0 else col
    lower = jnp.sum(jnp.where(below, counts, 0.0), axis=1 - axis, keepdims=True)
    lower = eye_turn(lower)
    count = jnp.sum(jnp.where(same, counts, 0.0), axis=1 - axis, keepdims=True)
    start = jnp.sum(jnp.where(same, lower, 0.0), axis=1 - axis, keepdims=True)
    line = lax.broadcasted_iota(jnp.int32, count.shape, axis)
    slot = (line - ((line * 171) >> 9) * SLOTS).astype(F32)
    index = jnp.where(slot < count, start + slot, -1.0)
    full = (LINES, ROWS) if axis == 0 else (ROWS, LINES)
    rows = lax.broadcasted_iota(jnp.int32, full, 1 - axis).astype(F32)
    return jnp.where(rows == index, 1.0, 0.0).astype(BF16)


def unstage(src, pick, write):
    for c in range(CHUNKS):
        rows = src[pl.ds(c, LINES, stride=CHUNKS), :].astype(BF16)
        write(slice(c * 128, (c + 1) * 128), matmul(pick[...], rows, 1, 0))


def unpack(recv, tiles):
    step = 4

    def some(i, carry):
        for j in range(step):
            k = i * step + j
            for t, halves in enumerate(tiles):
                tile = recv[k * len(tiles) + t].astype(F32)
                for h, (buffer, slot) in enumerate(halves):
                    off = pl.multiple_of((k * SLOTS + slot) * CHUNKS, CHUNKS)
                    buffer[pl.ds(off, CHUNKS), :] = tile[h * CHUNKS : (h + 1) * CHUNKS]
        return carry

    lax.fori_loop(0, PEERS // step, some, 0)


def wait_bytes(ref, sem):
    pltpu.make_async_copy(ref, ref, sem).wait()


def matmul(a, b, ca, cb):
    return lax.dot_general(a, b, (((ca,), (cb,)), ((), ())), preferred_element_type=F32)


def kernel(
    q_in, k_in, v_in, g_in, c_in, rel, lengths, pattern, counts,
    gq_out, gk_out, gv_out, gg_out, bias_out,
    send_0, send_1, send_2, send_3, send_4, send_5, recv_0, recv_1, recv_2, recv_3, recv_4, recv_5,
    stage_a, stage_b, send_out, send_in, settle, land, gn_low, n_low, gq_low, gk_low, gv_low,
    q_own, k_ext, v_ext, gn_own, inv, a_all, d_all, table, mask,
    o_all, go_all, gk_acc, gv_acc, halo_out, halo_in, gs_sum, part, red, cur,
    send_sem, recv_sem, halo_send, halo_recv, red_send, red_recv, ready,
):
    send = (send_0, send_1, send_2, send_3, send_4, send_5)
    recv = (recv_0, recv_1, recv_2, recv_3, recv_4, recv_5)
    me = lax.axis_index("ctx")
    grp = lax.axis_index("batch")
    x, z, y, c = coords(me)

    def ctx(i):
        return {"device_id": (grp, i), "device_id_type": MESH}

    barrier = pltpu.get_barrier_semaphore()
    line = [place(x, (z + d) % NZ, y, c) for d in range(1, NZ)]
    plane = [
        place((x + dx) % NX, z, (y + dy) % NY, (c + dc) % NC)
        for dx in range(NX) for dy in range(NY) for dc in range(NC)
    ][1:]
    for to in line + plane:
        pl.semaphore_signal(barrier, inc=1, **ctx(to))
    for d in range(1, BATCH):
        pl.semaphore_signal(barrier, inc=1, device_id=((grp + d) % BATCH, me), device_id_type=MESH)

    def exchange(group, tiles, staged, pick):
        out, into, n = send[group], recv[group], len(tiles)

        def pack(dst, k):
            for t, halves in enumerate(tiles):
                pieces = []
                for buffer, slot in halves:
                    off = pl.multiple_of((k * SLOTS + slot) * CHUNKS, CHUNKS)
                    pieces.append(buffer[pl.ds(off, CHUNKS), :])
                dst[k * n + t] = jnp.concatenate(pieces, axis=0).astype(BF16)

        def one(k, carry):
            pack(out, k)
            pltpu.make_async_remote_copy(
                src_ref=out.at[pl.ds(k * n, n)],
                dst_ref=into.at[pl.ds(k * n, n)],
                send_sem=send_sem.at[group],
                recv_sem=recv_sem.at[group],
                **ctx(partner(me, k)),
            ).start()
            return carry

        def stage(i):
            for buffer, value in staged:
                lines = pl.ds(pl.multiple_of(i * STEP * SLOTS, STEP * SLOTS), STEP * SLOTS)
                rows = matmul(pick[lines, :], value[...], 1, 0)
                for f in range(CHUNKS):
                    to = pl.ds(i * STEP * SLOTS * CHUNKS + f, STEP * SLOTS, stride=CHUNKS)
                    buffer[to, :] = rows[:, f * 128 : (f + 1) * 128]

        def chunk(i, carry):
            stage(i)
            return lax.fori_loop(i * STEP, i * STEP + STEP, one, carry)

        stage(0)
        lax.fori_loop(1, STEP, one, 0)
        pack(into, 0)
        lax.fori_loop(1, PEERS // STEP, chunk, 0)

    def arrived(group):
        n = recv[group].shape[0] // PEERS
        wait_bytes(recv[group].at[pl.ds(n, (PEERS - 1) * n)], recv_sem.at[group])

    def halo_copy(i, src, dst, to):
        return pltpu.make_async_remote_copy(
            src_ref=src, dst_ref=dst, send_sem=halo_send.at[i], recv_sem=halo_recv.at[i], **ctx(to)
        )

    out_row = counts[pl.ds(me, 1), :].astype(F32)
    lane = lax.broadcasted_iota(jnp.int32, (PEERS, PEERS), 1)
    in_col = jnp.sum(jnp.where(lane == me, counts[...].astype(F32), 0.0), axis=1, keepdims=True)
    out_col, in_row = eye_turn(out_row), eye_turn(in_col)
    send_out[...] = travel(me, out_row, out_col, 0, 1)

    gn_low[...] = (c_in[...].astype(F32) * g_in[...].astype(F32)).astype(BF16)
    pl.semaphore_wait(barrier, len(line) + len(plane) + BATCH - 1)
    for to in line:
        pl.semaphore_signal(ready, inc=1, **ctx(to))
    pl.semaphore_wait(ready, len(line))
    by_two = lambda a, b: (((a, 0), (b, 0)), ((a, 1), (b, 1)), ((a, 2), (b, 2)))
    exchange(0, by_two(stage_a, stage_b), ((stage_a, k_in), (stage_b, v_in)), send_out)
    rest = ((stage_b, 1), (stage_b, 2)),
    full = ((stage_a, 0), (stage_a, 1)), ((stage_a, 2), (stage_b, 0))
    exchange(1, full, ((stage_a, q_in), (stage_b, gn_low)), send_out)
    exchange(2, rest, (), send_out)
    settle[...] = travel(me, in_row, in_col, 1, -1)

    row_i = lax.broadcasted_iota(jnp.int32, (BLOCK, SPAN), 0)
    col_c = lax.broadcasted_iota(jnp.int32, (BLOCK, SPAN), 1)
    bucket = (row_i + BLOCK - col_c) >> 3

    def bias_of(h, carry):
        full = jnp.zeros((BLOCK, SPAN), F32)
        for k in range(BUCKETS):
            full = jnp.where(bucket == k, rel[h, k], full)
        table[h] = full
        return carry

    lax.fori_loop(0, HEADS, bias_of, 0)
    for b in range(2):
        pos_q = me * ROWS + b * BLOCK + row_i
        pos_k = me * ROWS + (b - 1) * BLOCK + col_c
        hist_q = jnp.zeros((BLOCK, SPAN), jnp.int32)
        hist_k = jnp.zeros((BLOCK, SPAN), jnp.int32)
        end = jnp.int32(0)
        for i in range(lengths.shape[1]):
            end = end + lengths[0, i]
            hist_q = hist_q + (pos_q >= end).astype(jnp.int32)
            hist_k = hist_k + (pos_k >= end).astype(jnp.int32)
        flag = jnp.where(col_c >= BLOCK, pattern[0, b, 0], pattern[0, b, 1])
        live = (pos_k <= pos_q) & (pos_k >= 0) & (hist_q == hist_k) & (flag > 0)
        mask[b] = jnp.where(live, 1.0 / SPAN, 0.0).astype(F32)

    def put_q(f, v):
        q_own[:, f] = v.astype(BF16)

    def put_k(f, v):
        k_ext[BLOCK:, f] = v.astype(BF16)

    def put_v(f, v):
        v_ext[BLOCK:, f] = v.astype(BF16)

    def put_gn(f, v):
        gn_own[:, f] = v

    after, before = (me + 1) % PEERS, (me + PEERS - 1) % PEERS
    arrived(0)
    unpack(recv[0], by_two(stage_a, stage_b))
    unstage(stage_a, settle, put_k)
    k_halo = halo_copy(0, k_ext.at[pl.ds(ROWS, BLOCK)], k_ext.at[pl.ds(0, BLOCK)], after)
    k_halo.start()
    unstage(stage_b, settle, put_v)
    v_halo = halo_copy(1, v_ext.at[pl.ds(ROWS, BLOCK)], v_ext.at[pl.ds(0, BLOCK)], after)
    v_halo.start()
    send_in[...] = travel(me, in_row, in_col, 0, 1)
    land[...] = travel(me, out_row, out_col, 1, -1)

    def forward(b):
        def one(h, carry):
            f = pl.ds(pl.multiple_of(h * SIZE, SIZE), SIZE)
            raw = matmul(q_own[pl.ds(b * BLOCK, BLOCK), f], k_ext[pl.ds(b * BLOCK, SPAN), f], 1, 1)
            s = raw * SCALE + table[h]
            sig = jax.nn.sigmoid(s)
            m = mask[b]
            a = (s * sig * m).astype(BF16)
            a_all[b, h] = a
            d_all[b, h] = sig * (1.0 + s * (1.0 - sig)) * m
            o_all[pl.ds(b * BLOCK, BLOCK), f] = matmul(a, v_ext[pl.ds(b * BLOCK, SPAN), f], 1, 0)
            return carry

        lax.fori_loop(0, HEADS, one, 0)

    arrived(1)
    unpack(recv[1], full)
    unstage(stage_a, settle, put_q)
    forward(1)
    k_halo.wait_recv()
    v_halo.wait_recv()
    forward(0)

    def norm(i, carry):
        rows = pl.ds(pl.multiple_of(i * 32, 32), 32)
        out = o_all[rows, :]
        center = out - jnp.mean(out, axis=-1, keepdims=True)
        inverse = lax.rsqrt(jnp.mean(center * center, axis=-1, keepdims=True) + EPS)
        normed = center * inverse
        o_all[rows, :] = normed
        n_low[rows, :] = normed.astype(BF16)
        inv[rows, :] = jnp.broadcast_to(inverse, (32, 128))
        return carry

    lax.fori_loop(0, ROWS // 32, norm, 0)
    exchange(3, (((stage_a, 0), (stage_a, 1)),), ((stage_a, n_low),), send_in)

    arrived(2)
    unpack(recv[2], rest)
    unstage(stage_b, settle, put_gn)

    def norm_back(i, carry):
        rows = pl.ds(pl.multiple_of(i * 32, 32), 32)
        normed = o_all[rows, :]
        gn = gn_own[rows, :]
        go = (
            gn
            - jnp.mean(gn, axis=-1, keepdims=True)
            - normed * jnp.mean(gn * normed, axis=-1, keepdims=True)
        ) * inv[rows, :1]
        go_all[rows, :] = go.astype(BF16)
        return carry

    lax.fori_loop(0, ROWS // 32, norm_back, 0)

    def back(b):
        def one(h, carry):
            f = pl.ds(pl.multiple_of(h * SIZE, SIZE), SIZE)
            own = pl.ds(b * BLOCK, BLOCK)
            win = pl.ds(b * BLOCK, SPAN)
            go = go_all[own, f]
            gs = matmul(go, v_ext[win, f], 1, 1) * d_all[b, h]
            low = gs.astype(BF16)
            gq_low[own, f] = (matmul(low, k_ext[win, f], 1, 0) * SCALE).astype(BF16)
            gk = matmul(low, q_own[own, f], 0, 0) * SCALE
            gv = matmul(a_all[b, h], go, 0, 0)
            if b == 0:
                gs_sum[h] = gs
                halo_out[0, :, f] = gk[:BLOCK].astype(BF16)
                halo_out[1, :, f] = gv[:BLOCK].astype(BF16)
                gk_acc[pl.ds(0, BLOCK), f] = gk[BLOCK:]
                gv_acc[pl.ds(0, BLOCK), f] = gv[BLOCK:]
            else:
                gs_sum[h] += gs
                gk_acc[pl.ds(0, BLOCK), f] += gk[:BLOCK]
                gv_acc[pl.ds(0, BLOCK), f] += gv[:BLOCK]
                gk_acc[pl.ds(BLOCK, BLOCK), f] = gk[BLOCK:]
                gv_acc[pl.ds(BLOCK, BLOCK), f] = gv[BLOCK:]
            return carry

        lax.fori_loop(0, HEADS, one, 0)

    back(0)
    g_halo = halo_copy(2, halo_out, halo_in, before)
    g_halo.start()
    back(1)

    mixed = ((stage_a, 2), (stage_b, 0)), ((stage_b, 1), (stage_b, 2))
    exchange(4, mixed, ((stage_b, gq_low),), send_in)

    def buckets_of(h, carry):
        gs = gs_sum[h]
        for k in range(BUCKETS):
            picked = jnp.where(bucket == k, gs, 0.0)
            part[pl.ds(h * BUCKETS + k, 1), :] = jnp.sum(picked, axis=0, keepdims=True)
        return carry

    lax.fori_loop(0, HEADS, buckets_of, 0)
    sums = jnp.sum(part[...], axis=1, keepdims=True)
    lines = [eye_turn(sums[r * 128 : (r + 1) * 128]) for r in range(2)]
    first_total = jnp.concatenate(lines + [jnp.zeros((6, 128), F32)], axis=0)

    rounds = (
        (NY * NC, y * NC + c, lambda i: (grp, place(x, z, i // NC, i % NC))),
        (NZ, z, lambda i: (grp, place(x, i, y, c))),
        (NX, x, lambda i: (grp, place(i, z, y, c))),
        (BATCH, grp, lambda i: (i, me)),
    )

    def round_start(r, value):
        n, mine, device = rounds[r]
        cur[r] = value
        red[r, mine] = value
        for d in range(1, n):
            pltpu.make_async_remote_copy(
                src_ref=cur.at[r],
                dst_ref=red.at[r, mine],
                send_sem=red_send.at[r],
                recv_sem=red_recv.at[r],
                device_id=device((mine + d) % n),
                device_id_type=MESH,
            ).start()

    def round_end(r):
        n = rounds[r][0]
        wait_bytes(red.at[r, pl.ds(0, n - 1)], red_recv.at[r])
        total = red[r, 0]
        for i in range(1, n):
            total = total + red[r, i]
        return total

    round_start(0, first_total)

    g_halo.wait_recv()
    for acc, low, i in ((gk_acc, gk_low, 0), (gv_acc, gv_low, 1)):
        low[:BLOCK, :] = acc[:BLOCK, :].astype(BF16)
        low[BLOCK:, :] = (acc[BLOCK:, :] + halo_in[i].astype(F32)).astype(BF16)
    exchange(5, by_two(stage_a, stage_b), ((stage_a, gk_low), (stage_b, gv_low)), send_in)

    round_start(1, round_end(0))
    round_start(2, round_end(1))
    def put_gate(f, v):
        gg_out[:, f] = (c_in[:, f].astype(F32) * v).astype(BF16)

    def put_gq(f, v):
        gq_out[:, f] = v.astype(BF16)

    def put_gk(f, v):
        gk_out[:, f] = v.astype(BF16)

    def put_gv(f, v):
        gv_out[:, f] = v.astype(BF16)

    arrived(3)
    unpack(recv[3], (((stage_a, 0), (stage_a, 1)),))
    arrived(4)
    unpack(recv[4], mixed)
    unstage(stage_a, land, put_gate)
    unstage(stage_b, land, put_gq)
    round_start(3, round_end(2))
    total = round_end(3) * (1.0 / math.sqrt(BATCH * PEERS * ROWS))
    for h in range(HEADS):
        at = h % 4 * BUCKETS
        bias_out[h : h + 1, :] = total[h // 4 : h // 4 + 1, at : at + BUCKETS]

    arrived(5)
    unpack(recv[5], by_two(stage_a, stage_b))
    unstage(stage_a, land, put_gk)
    unstage(stage_b, land, put_gv)

    for group in range(6):
        n = send[group].shape[0] // PEERS
        wait_bytes(send[group].at[pl.ds(n, (PEERS - 1) * n)], send_sem.at[group])
    k_halo.wait_send()
    v_halo.wait_send()
    g_halo.wait_send()
    for r in range(4):
        wait_bytes(red.at[r, pl.ds(0, rounds[r][0] - 1)], red_send.at[r])


def body(queries, keys, values, gates, cotangent, rel_bias, lengths, send_counts, block_pattern):
    vmem = pl.BlockSpec(memory_space=pltpu.VMEM)
    smem = pl.BlockSpec(memory_space=pltpu.SMEM)
    event = jax.ShapeDtypeStruct((ROWS, WIDTH), BF16)
    wide = pltpu.VMEM((ROWS, WIDTH), F32)
    low = pltpu.VMEM((ROWS, WIDTH), BF16)
    stage = pltpu.VMEM((LINES * CHUNKS, 128), F32)
    buffers = [pltpu.VMEM((PEERS * n, 16, 128), BF16) for n in (3, 2, 1, 1, 2, 3)]
    gq, gk, gv, gg, bias = pl.pallas_call(
        kernel,
        out_shape=(event, event, event, event, jax.ShapeDtypeStruct((HEADS, BUCKETS), F32)),
        in_specs=[vmem] * 5 + [smem] * 3 + [vmem],
        out_specs=(vmem,) * 5,
        scratch_shapes=buffers * 2
        + [stage, stage]
        + [pltpu.VMEM((LINES, ROWS), BF16)] * 2
        + [pltpu.VMEM((ROWS, LINES), BF16)] * 2
        + [low] * 5
        + [low, pltpu.VMEM((ROWS + BLOCK, WIDTH), BF16), pltpu.VMEM((ROWS + BLOCK, WIDTH), BF16), wide]
        + [
            pltpu.VMEM((ROWS, 128), F32),
            pltpu.VMEM((2, HEADS, BLOCK, SPAN), BF16),
            pltpu.VMEM((2, HEADS, BLOCK, SPAN), F32),
            pltpu.VMEM((HEADS, BLOCK, SPAN), F32),
            pltpu.VMEM((2, BLOCK, SPAN), F32),
        ]
        + [wide, low, wide, wide]
        + [
            pltpu.VMEM((2, BLOCK, WIDTH), BF16),
            pltpu.VMEM((2, BLOCK, WIDTH), BF16),
            pltpu.VMEM((HEADS, BLOCK, SPAN), F32),
            pltpu.VMEM((HEADS * BUCKETS, SPAN), F32),
            pltpu.VMEM((4, 8, 8, 128), F32),
            pltpu.VMEM((4, 8, 128), F32),
            pltpu.SemaphoreType.DMA((6,)),
            pltpu.SemaphoreType.DMA((6,)),
            pltpu.SemaphoreType.DMA((3,)),
            pltpu.SemaphoreType.DMA((3,)),
            pltpu.SemaphoreType.DMA((4,)),
            pltpu.SemaphoreType.DMA((4,)),
            pltpu.SemaphoreType.REGULAR,
        ],
        compiler_params=pltpu.CompilerParams(
            collective_id=0, has_side_effects=True, vmem_limit_bytes=56 * 1024 * 1024
        ),
    )(
        queries[0], keys[0], values[0], gates[0], cotangent[0],
        rel_bias, lengths, block_pattern, send_counts[0],
    )
    return gq[None], gk[None], gv[None], gg[None], bias


def solution(mesh):
    event = P("batch", "ctx", None)
    return jax.shard_map(
        body,
        mesh=mesh,
        in_specs=(event,) * 5 + (P(), P("batch", None), P("batch", None, None), event),
        out_specs=(event,) * 4 + (P(),),
        check_vma=False,
    )
```

time: 209 us -> 194 us (0.928)
  Pallas kernels: 195 us -> 187 us
  local copies, waits for them, and re-layouts: 11.8 us -> 5.78 us
    pallas_call x1, Pallas kernels: 195 us -> 187 us  [body(): pl.pallas_call(kernel, out_shape=(event, event, event, event, jax.ShapeDt...]
    select_n x4 -> x0, local copies, waits for them, and re-layouts: 3.1 us -> none  [ordered(): jnp.where(slot[None, :] < count[:, None], start[:, None] + slot[None, :],...]
    unnamed x14 -> x13, local copies, waits for them, and re-layouts: 6.59 us -> 5.78 us
where the time goes in v2:
time: 194 us; the launch traced here: 193 us
  Pallas kernels  187 us (96%)
  local copies, waits for them, and re-layouts  5.78 us (3%)
    pallas_call x1, Pallas kernels, body(): pl.pallas_call(kernel, out_shape=(event, event, event, event, jax.ShapeDt...  187 us
    unnamed x13, local copies, waits for them, and re-layouts  5.78 us

profile of v2, /device:TPU:8, one launch (start us, length us, event | category | flops | bytes accessed | tf_op | source)
XLA Modules:
  0.0 193.3 jit_solution(8437024996978880373)
XLA Ops:
  0.6 186.9 %shard_map.128 = (bf16[256,1024]{1,0:T(8,128)(2,1)}, bf16[256,1024]{1,0:T(8,128)(2,1)}, bf16[256,1024]{1,0:T(8,128)(2,1)}, bf16[256,1024]{1,0:T(8,128)(2,1)}, f32[8,32]{1,0:T(8,128)}) custom-call(bf16[256,1024]{1,0:T(8,128)(2,1)} %bitcast.14, bf16[256,1024]{1,0:T(8,128)(2,1)} %bitcast.15, bf16[256,1024]{1,0:T(8,128)(2,1)} %bitcast.16, ...), custom_call_target="tpu_custom_call" | custom-call | tf_op jit(solution)/shard_map/pallas_call | solution.py:442
  187.6 0.0 copy-start.2
  187.6 1.9 copy.19
  189.5 0.0 copy-done.2
  189.5 0.0 copy-start.1
  189.5 0.8 copy.20
  190.3 0.4 copy-done.1
  190.7 0.0 copy-start
  190.7 0.8 copy.21
  191.5 0.4 copy-done
  192.0 0.0 copy-start.3
  192.0 0.8 copy.22
  192.7 0.0 copy-done.3
  192.8 0.6 copy.23
Async XLA Ops:
  187.6 1.9 %copy-start.2 = (bf16[256,1024]{1,0:T(8,128)(2,1)S(1)}, bf16[256,1024]{1,0:T(8,128)(2,1)}, u32[]{:S(2)}) copy-start(bf16[256,1024]{1,0:T(8,128)(2,1)} %get-tuple-element.11) | copy-start | bytes 1572868
  189.5 1.2 copy-start.1
  190.7 1.2 copy-start
  192.0 0.8 copy-start.3

commit v3 on v2

--- a/solution.py
+++ b/solution.py
@@ -24,6 +24,7 @@
 BUCKETS = 32
 SLOTS = 3
 EPS = 1e-05
+VMEM = 56 * 1024 * 1024
 LINES = PEERS * SLOTS
 STEP = 16
 SCALE = SIZE ** (-0.5)
@@ -54,12 +55,15 @@
     return jnp.sum(jnp.where(eye, vector, 0.0), axis=1 if vector.shape[0] == 1 else 0, keepdims=True)
 
 
-def travel(me, row, col, axis, sign):
-    shape = (LINES, 128) if axis == 0 else (128, LINES)
+def travel(me, row, col, axis, sign, only=None):
+    def offset(line):
+        return (line * 171) >> 9 if only is None else line
+
+    lines = LINES if only is None else PEERS
+    shape = (lines, 128) if axis == 0 else (128, lines)
     device = lax.broadcasted_iota(jnp.int32, shape, 1 - axis)
     along = lax.broadcasted_iota(jnp.int32, shape, axis)
-    k = (along * 171) >> 9
-    same = partners_of(me, k, sign) == device
+    same = partners_of(me, offset(along), sign) == device
     pairs = (128, 128)
     below = lax.broadcasted_iota(jnp.int32, pairs, 1 - axis) < lax.broadcasted_iota(jnp.int32, pairs, axis)
     counts = row if axis == 0 else col
@@ -68,20 +72,20 @@
     count = jnp.sum(jnp.where(same, counts, 0.0), axis=1 - axis, keepdims=True)
     start = jnp.sum(jnp.where(same, lower, 0.0), axis=1 - axis, keepdims=True)
     line = lax.broadcasted_iota(jnp.int32, count.shape, axis)
-    slot = (line - ((line * 171) >> 9) * SLOTS).astype(F32)
+    slot = (line - offset(line) * SLOTS).astype(F32) if only is None else float(only)
     index = jnp.where(slot < count, start + slot, -1.0)
-    full = (LINES, ROWS) if axis == 0 else (ROWS, LINES)
+    full = (lines, ROWS) if axis == 0 else (ROWS, lines)
     rows = lax.broadcasted_iota(jnp.int32, full, 1 - axis).astype(F32)
     return jnp.where(rows == index, 1.0, 0.0).astype(BF16)
 
 
 def unstage(src, pick, write):
     for c in range(CHUNKS):
-        rows = src[pl.ds(c, LINES, stride=CHUNKS), :].astype(BF16)
+        rows = src[pl.ds(c, pick.shape[1], stride=CHUNKS), :].astype(BF16)
         write(slice(c * 128, (c + 1) * 128), matmul(pick[...], rows, 1, 0))
 
 
-def unpack(recv, tiles):
+def unpack(recv, tiles, slots=SLOTS):
     step = 4
 
     def some(i, carry):
@@ -90,7 +94,7 @@
             for t, halves in enumerate(tiles):
                 tile = recv[k * len(tiles) + t].astype(F32)
                 for h, (buffer, slot) in enumerate(halves):
-                    off = pl.multiple_of((k * SLOTS + slot) * CHUNKS, CHUNKS)
+                    off = pl.multiple_of((k * slots + slot) * CHUNKS, CHUNKS)
                     buffer[pl.ds(off, CHUNKS), :] = tile[h * CHUNKS : (h + 1) * CHUNKS]
         return carry
 
@@ -106,16 +110,18 @@
 
 
 def kernel(
-    q_in, k_in, v_in, g_in, c_in, rel, lengths, pattern, counts,
-    gq_out, gk_out, gv_out, gg_out, bias_out,
-    send_0, send_1, send_2, send_3, send_4, send_5, recv_0, recv_1, recv_2, recv_3, recv_4, recv_5,
-    stage_a, stage_b, send_out, send_in, settle, land, gn_low, n_low, gq_low, gk_low, gv_low,
+    q_hbm, k_hbm, v_hbm, g_hbm, c_hbm, rel, lengths, pattern, counts,
+    gq_hbm, gk_hbm, gv_hbm, gg_hbm, bias_out,
+    send_0, send_1, send_2, send_3, send_4, send_5, send_6,
+    recv_0, recv_1, recv_2, recv_3, recv_4, recv_5, recv_6,
+    q_in, k_in, v_in, g_in, c_in, gq_out, gk_out, gv_out, gg_out,
+    stage_a, stage_b, send_out, send_in, settle, land, land_last, gn_low, n_low, gq_low, gk_low, gv_low,
     q_own, k_ext, v_ext, gn_own, inv, a_all, d_all, table, mask,
     o_all, go_all, gk_acc, gv_acc, halo_out, halo_in, gs_sum, part, red, cur,
-    send_sem, recv_sem, halo_send, halo_recv, red_send, red_recv, ready,
+    send_sem, recv_sem, halo_send, halo_recv, red_send, red_recv, ready, in_sem, out_sem,
 ):
-    send = (send_0, send_1, send_2, send_3, send_4, send_5)
-    recv = (recv_0, recv_1, recv_2, recv_3, recv_4, recv_5)
+    send = (send_0, send_1, send_2, send_3, send_4, send_5, send_6)
+    recv = (recv_0, recv_1, recv_2, recv_3, recv_4, recv_5, recv_6)
     me = lax.axis_index("ctx")
     grp = lax.axis_index("batch")
     x, z, y, c = coords(me)
@@ -134,7 +140,21 @@
     for d in range(1, BATCH):
         pl.semaphore_signal(barrier, inc=1, device_id=((grp + d) % BATCH, me), device_id_type=MESH)
 
-    def exchange(group, tiles, staged, pick):
+    loads = [
+        pltpu.make_async_copy(src, dst, in_sem.at[i])
+        for i, (src, dst) in enumerate(
+            ((k_hbm, k_in), (v_hbm, v_in), (c_hbm, c_in), (g_hbm, g_in), (q_hbm, q_in))
+        )
+    ]
+    for load in loads:
+        load.start()
+
+    def leave(i, src, dst):
+        copy = pltpu.make_async_copy(src, dst, out_sem.at[i])
+        copy.start()
+        return copy
+
+    def exchange(group, tiles, staged, pick, gate=None):
         out, into, n = send[group], recv[group], len(tiles)
 
         def pack(dst, k):
@@ -169,6 +189,8 @@
             return lax.fori_loop(i * STEP, i * STEP + STEP, one, carry)
 
         stage(0)
+        if gate is not None:
+            gate()
         lax.fori_loop(1, STEP, one, 0)
         pack(into, 0)
         lax.fori_loop(1, PEERS // STEP, chunk, 0)
@@ -181,6 +203,10 @@
         return pltpu.make_async_remote_copy(
             src_ref=src, dst_ref=dst, send_sem=halo_send.at[i], recv_sem=halo_recv.at[i], **ctx(to)
         )
+
+    pl.semaphore_wait(barrier, len(line) + len(plane) + BATCH - 1)
+    for to in line:
+        pl.semaphore_signal(ready, inc=1, **ctx(to))
 
     out_row = counts[pl.ds(me, 1), :].astype(F32)
     lane = lax.broadcasted_iota(jnp.int32, (PEERS, PEERS), 1)
@@ -188,13 +214,14 @@
     out_col, in_row = eye_turn(out_row), eye_turn(in_col)
     send_out[...] = travel(me, out_row, out_col, 0, 1)
 
+    by_two = lambda a, b: (((a, 0), (b, 0)), ((a, 1), (b, 1)), ((a, 2), (b, 2)))
+    loads[0].wait()
+    loads[1].wait()
+    everyone = lambda: pl.semaphore_wait(ready, len(line))
+    exchange(0, by_two(stage_a, stage_b), ((stage_a, k_in), (stage_b, v_in)), send_out, everyone)
+    for load in loads[2:]:
+        load.wait()
     gn_low[...] = (c_in[...].astype(F32) * g_in[...].astype(F32)).astype(BF16)
-    pl.semaphore_wait(barrier, len(line) + len(plane) + BATCH - 1)
-    for to in line:
-        pl.semaphore_signal(ready, inc=1, **ctx(to))
-    pl.semaphore_wait(ready, len(line))
-    by_two = lambda a, b: (((a, 0), (b, 0)), ((a, 1), (b, 1)), ((a, 2), (b, 2)))
-    exchange(0, by_two(stage_a, stage_b), ((stage_a, k_in), (stage_b, v_in)), send_out)
     rest = ((stage_b, 1), (stage_b, 2)),
     full = ((stage_a, 0), (stage_a, 1)), ((stage_a, 2), (stage_b, 0))
     exchange(1, full, ((stage_a, q_in), (stage_b, gn_low)), send_out)
@@ -250,6 +277,7 @@
     v_halo.start()
     send_in[...] = travel(me, in_row, in_col, 0, 1)
     land[...] = travel(me, out_row, out_col, 1, -1)
+    land_last[...] = travel(me, out_row, out_col, 1, -1, SLOTS - 1)
 
     def forward(b):
         def one(h, carry):
@@ -264,7 +292,7 @@
             o_all[pl.ds(b * BLOCK, BLOCK), f] = matmul(a, v_ext[pl.ds(b * BLOCK, SPAN), f], 1, 0)
             return carry
 
-        lax.fori_loop(0, HEADS, one, 0)
+        lax.fori_loop(0, HEADS, one, 0, unroll=2)
 
     arrived(1)
     unpack(recv[1], full)
@@ -331,7 +359,7 @@
                 gv_acc[pl.ds(BLOCK, BLOCK), f] = gv[BLOCK:]
             return carry
 
-        lax.fori_loop(0, HEADS, one, 0)
+        lax.fori_loop(0, HEADS, one, 0, unroll=2)
 
     back(0)
     g_halo = halo_copy(2, halo_out, halo_in, before)
@@ -388,7 +416,9 @@
     for acc, low, i in ((gk_acc, gk_low, 0), (gv_acc, gv_low, 1)):
         low[:BLOCK, :] = acc[:BLOCK, :].astype(BF16)
         low[BLOCK:, :] = (acc[BLOCK:, :] + halo_in[i].astype(F32)).astype(BF16)
-    exchange(5, by_two(stage_a, stage_b), ((stage_a, gk_low), (stage_b, gv_low)), send_in)
+    first_two = by_two(stage_a, stage_b)[:2]
+    exchange(5, first_two, ((stage_a, gk_low), (stage_b, gv_low)), send_in)
+    exchange(6, by_two(stage_a, stage_b)[2:], (), send_in)
 
     round_start(1, round_end(0))
     round_start(2, round_end(1))
@@ -399,17 +429,28 @@
         gq_out[:, f] = v.astype(BF16)
 
     def put_gk(f, v):
-        gk_out[:, f] = v.astype(BF16)
+        gk_acc[:, f] = v
 
     def put_gv(f, v):
-        gv_out[:, f] = v.astype(BF16)
+        gv_acc[:, f] = v
+
+    def end_gk(f, v):
+        gk_out[:, f] = (gk_acc[:, f] + v).astype(BF16)
+
+    def end_gv(f, v):
+        gv_out[:, f] = (gv_acc[:, f] + v).astype(BF16)
 
     arrived(3)
     unpack(recv[3], (((stage_a, 0), (stage_a, 1)),))
     arrived(4)
     unpack(recv[4], mixed)
     unstage(stage_a, land, put_gate)
+    gone = [leave(0, gg_out, gg_hbm)]
     unstage(stage_b, land, put_gq)
+    gone.append(leave(1, gq_out, gq_hbm))
+    lines = lax.broadcasted_iota(jnp.int32, (ROWS, LINES), 1)
+    early = lines - ((lines * 171) >> 9) * SLOTS < SLOTS - 1
+    land[...] = jnp.where(early, land[...].astype(F32), 0.0).astype(BF16)
     round_start(3, round_end(2))
     total = round_end(3) * (1.0 / math.sqrt(BATCH * PEERS * ROWS))
     for h in range(HEADS):
@@ -417,11 +458,19 @@
         bias_out[h : h + 1, :] = total[h // 4 : h // 4 + 1, at : at + BUCKETS]
 
     arrived(5)
-    unpack(recv[5], by_two(stage_a, stage_b))
+    unpack(recv[5], first_two)
     unstage(stage_a, land, put_gk)
     unstage(stage_b, land, put_gv)
-
-    for group in range(6):
+    arrived(6)
+    unpack(recv[6], (((stage_a, 0), (stage_b, 0)),), 1)
+    unstage(stage_a, land_last, end_gk)
+    gone.append(leave(2, gk_out, gk_hbm))
+    unstage(stage_b, land_last, end_gv)
+    gone.append(leave(3, gv_out, gv_hbm))
+
+    for copy in gone:
+        copy.wait()
+    for group in range(7):
         n = send[group].shape[0] // PEERS
         wait_bytes(send[group].at[pl.ds(n, (PEERS - 1) * n)], send_sem.at[group])
     k_halo.wait_send()
@@ -431,23 +480,31 @@
         wait_bytes(red.at[r, pl.ds(0, rounds[r][0] - 1)], red_send.at[r])
 
 
+def hand_over(*refs):
+    for i in range(5):
+        refs[5 + i][...] = refs[i][...]
+
+
 def body(queries, keys, values, gates, cotangent, rel_bias, lengths, send_counts, block_pattern):
     vmem = pl.BlockSpec(memory_space=pltpu.VMEM)
     smem = pl.BlockSpec(memory_space=pltpu.SMEM)
+    hbm = pl.BlockSpec(memory_space=pl.ANY)
     event = jax.ShapeDtypeStruct((ROWS, WIDTH), BF16)
     wide = pltpu.VMEM((ROWS, WIDTH), F32)
     low = pltpu.VMEM((ROWS, WIDTH), BF16)
     stage = pltpu.VMEM((LINES * CHUNKS, 128), F32)
-    buffers = [pltpu.VMEM((PEERS * n, 16, 128), BF16) for n in (3, 2, 1, 1, 2, 3)]
-    gq, gk, gv, gg, bias = pl.pallas_call(
+    buffers = [pltpu.VMEM((PEERS * n, 16, 128), BF16) for n in (3, 2, 1, 1, 2, 2, 1)]
+    results = pl.pallas_call(
         kernel,
         out_shape=(event, event, event, event, jax.ShapeDtypeStruct((HEADS, BUCKETS), F32)),
-        in_specs=[vmem] * 5 + [smem] * 3 + [vmem],
-        out_specs=(vmem,) * 5,
+        in_specs=[hbm] * 5 + [smem] * 3 + [vmem],
+        out_specs=(hbm,) * 4 + (vmem,),
         scratch_shapes=buffers * 2
+        + [low] * 9
         + [stage, stage]
         + [pltpu.VMEM((LINES, ROWS), BF16)] * 2
         + [pltpu.VMEM((ROWS, LINES), BF16)] * 2
+        + [pltpu.VMEM((ROWS, PEERS), BF16)]
         + [low] * 5
         + [low, pltpu.VMEM((ROWS + BLOCK, WIDTH), BF16), pltpu.VMEM((ROWS + BLOCK, WIDTH), BF16), wide]
         + [
@@ -465,21 +522,33 @@
             pltpu.VMEM((HEADS * BUCKETS, SPAN), F32),
             pltpu.VMEM((4, 8, 8, 128), F32),
             pltpu.VMEM((4, 8, 128), F32),
-            pltpu.SemaphoreType.DMA((6,)),
-            pltpu.SemaphoreType.DMA((6,)),
+            pltpu.SemaphoreType.DMA((7,)),
+            pltpu.SemaphoreType.DMA((7,)),
             pltpu.SemaphoreType.DMA((3,)),
             pltpu.SemaphoreType.DMA((3,)),
             pltpu.SemaphoreType.DMA((4,)),
             pltpu.SemaphoreType.DMA((4,)),
             pltpu.SemaphoreType.REGULAR,
+            pltpu.SemaphoreType.DMA((5,)),
+            pltpu.SemaphoreType.DMA((4,)),
         ],
         compiler_params=pltpu.CompilerParams(
-            collective_id=0, has_side_effects=True, vmem_limit_bytes=56 * 1024 * 1024
+            collective_id=0, has_side_effects=True, vmem_limit_bytes=VMEM
         ),
     )(
         queries[0], keys[0], values[0], gates[0], cotangent[0],
         rel_bias, lengths, block_pattern, send_counts[0],
     )
+    strips = [pl.BlockSpec((ROWS // 4, WIDTH), lambda i: (i, 0))] * 4
+    strips.append(pl.BlockSpec((HEADS, BUCKETS), lambda i: (0, 0)))
+    gq, gk, gv, gg, bias = pl.pallas_call(
+        hand_over,
+        out_shape=[jax.ShapeDtypeStruct(r.shape, r.dtype) for r in results],
+        grid=(4,),
+        in_specs=strips,
+        out_specs=strips,
+        compiler_params=pltpu.CompilerParams(vmem_limit_bytes=VMEM),
+    )(*results)
     return gq[None], gk[None], gv[None], gg[None], bias
 
 

time: 194 us -> 188 us (0.969)
  local copies, waits for them, and re-layouts: 5.78 us -> 0 us
    unnamed x13 -> x0, local copies, waits for them, and re-layouts: 5.78 us -> none
    pallas_call x0 -> x1, Pallas kernels: none -> 3.81 us  [body(): pl.pallas_call(hand_over, out_shape=[jax.ShapeDtypeStruct(r.shape, r.dtyp...]
    pallas_call x1, Pallas kernels: 187 us -> 184 us  [body(): pl.pallas_call(kernel, out_shape=(event, event, event, event, jax.ShapeDt...]
where the time goes in v3:
time: 188 us
  Pallas kernels  187 us (99%)
    pallas_call x1, Pallas kernels, body(): pl.pallas_call(kernel, out_shape=(event, event, event, event, jax.ShapeDt...  184 us
    pallas_call x1, Pallas kernels, body(): pl.pallas_call(hand_over, out_shape=[jax.ShapeDtypeStruct(r.shape, r.dtyp...  3.81 us

profile of v3, /device:TPU:8, one launch (start us, length us, event | category | flops | bytes accessed | tf_op | source)
XLA Modules:
  0.0 188.0 jit_solution(7418772208117760912)
XLA Ops:
  0.6 183.5 %shard_map.128 = (bf16[256,1024]{1,0:T(8,128)(2,1)}, bf16[256,1024]{1,0:T(8,128)(2,1)}, bf16[256,1024]{1,0:T(8,128)(2,1)}, bf16[256,1024]{1,0:T(8,128)(2,1)}, f32[8,32]{1,0:T(8,128)}) custom-call(bf16[256,1024]{1,0:T(8,128)(2,1)} %bitcast.10, bf16[256,1024]{1,0:T(8,128)(2,1)} %bitcast.11, bf16[256,1024]{1,0:T(8,128)(2,1)} %bitcast.12, ...), custom_call_target="tpu_custom_call" | custom-call | tf_op jit(solution)/shard_map/pallas_call | solution.py:497
  184.2 3.8 %shard_map.129 = (bf16[256,1024]{1,0:T(8,128)(2,1)}, bf16[256,1024]{1,0:T(8,128)(2,1)}, bf16[256,1024]{1,0:T(8,128)(2,1)}, bf16[256,1024]{1,0:T(8,128)(2,1)}, f32[8,32]{1,0:T(8,128)}) custom-call(bf16[256,1024]{1,0:T(8,128)(2,1)} %get-tuple-element.15.refs_0_, bf16[256,1024]{1,0:T(8,128)(2,1)} %get-tuple-element.16.refs_1_, ...), custom_call_target="tpu_custom_call" | custom-call | tf_op jit(solution)/shard_map/pallas_call | solution.py:544

commit v4 on v3

--- a/solution.py
+++ b/solution.py
@@ -292,7 +292,7 @@
             o_all[pl.ds(b * BLOCK, BLOCK), f] = matmul(a, v_ext[pl.ds(b * BLOCK, SPAN), f], 1, 0)
             return carry
 
-        lax.fori_loop(0, HEADS, one, 0, unroll=2)
+        lax.fori_loop(0, HEADS, one, 0, unroll=4)
 
     arrived(1)
     unpack(recv[1], full)
@@ -313,7 +313,7 @@
         inv[rows, :] = jnp.broadcast_to(inverse, (32, 128))
         return carry
 
-    lax.fori_loop(0, ROWS // 32, norm, 0)
+    lax.fori_loop(0, ROWS // 32, norm, 0, unroll=2)
     exchange(3, (((stage_a, 0), (stage_a, 1)),), ((stage_a, n_low),), send_in)
 
     arrived(2)
@@ -332,7 +332,7 @@
         go_all[rows, :] = go.astype(BF16)
         return carry
 
-    lax.fori_loop(0, ROWS // 32, norm_back, 0)
+    lax.fori_loop(0, ROWS // 32, norm_back, 0, unroll=2)
 
     def back(b):
         def one(h, carry):
@@ -359,7 +359,7 @@
                 gv_acc[pl.ds(BLOCK, BLOCK), f] = gv[BLOCK:]
             return carry
 
-        lax.fori_loop(0, HEADS, one, 0, unroll=2)
+        lax.fori_loop(0, HEADS, one, 0, unroll=4)
 
     back(0)
     g_halo = halo_copy(2, halo_out, halo_in, before)
@@ -539,12 +539,12 @@
         queries[0], keys[0], values[0], gates[0], cotangent[0],
         rel_bias, lengths, block_pattern, send_counts[0],
     )
-    strips = [pl.BlockSpec((ROWS // 4, WIDTH), lambda i: (i, 0))] * 4
+    strips = [pl.BlockSpec((ROWS // 2, WIDTH), lambda i: (i, 0))] * 4
     strips.append(pl.BlockSpec((HEADS, BUCKETS), lambda i: (0, 0)))
     gq, gk, gv, gg, bias = pl.pallas_call(
         hand_over,
         out_shape=[jax.ShapeDtypeStruct(r.shape, r.dtype) for r in results],
-        grid=(4,),
+        grid=(2,),
         in_specs=strips,
         out_specs=strips,
         compiler_params=pltpu.CompilerParams(vmem_limit_bytes=VMEM),

time: 188 us -> 184 us (0.979)
  Pallas kernels: 187 us -> 183 us
    pallas_call x1, Pallas kernels: 184 us -> 181 us  [body(): pl.pallas_call(kernel, out_shape=(event, event, event, event, jax.ShapeDt...]
where the time goes in v4:
time: 184 us
  Pallas kernels  183 us (99%)
    pallas_call x1, Pallas kernels, body(): pl.pallas_call(kernel, out_shape=(event, event, event, event, jax.ShapeDt...  181 us

profile of v4, /device:TPU:8, one launch (start us, length us, event | category | flops | bytes accessed | tf_op | source)
XLA Modules:
  0.0 184.1 jit_solution(7218158107145813384)
XLA Ops:
  0.6 180.9 %shard_map.128 = (bf16[256,1024]{1,0:T(8,128)(2,1)}, bf16[256,1024]{1,0:T(8,128)(2,1)}, bf16[256,1024]{1,0:T(8,128)(2,1)}, bf16[256,1024]{1,0:T(8,128)(2,1)}, f32[8,32]{1,0:T(8,128)}) custom-call(bf16[256,1024]{1,0:T(8,128)(2,1)} %bitcast.10, bf16[256,1024]{1,0:T(8,128)(2,1)} %bitcast.11, bf16[256,1024]{1,0:T(8,128)(2,1)} %bitcast.12, ...), custom_call_target="tpu_custom_call" | custom-call | tf_op jit(solution)/shard_map/pallas_call | solution.py:497
  181.5 2.6 %shard_map.129 = (bf16[256,1024]{1,0:T(8,128)(2,1)}, bf16[256,1024]{1,0:T(8,128)(2,1)}, bf16[256,1024]{1,0:T(8,128)(2,1)}, bf16[256,1024]{1,0:T(8,128)(2,1)}, f32[8,32]{1,0:T(8,128)}) custom-call(bf16[256,1024]{1,0:T(8,128)(2,1)} %get-tuple-element.15.refs_0_, bf16[256,1024]{1,0:T(8,128)(2,1)} %get-tuple-element.16.refs_1_, ...), custom_call_target="tpu_custom_call" | custom-call | tf_op jit(solution)/shard_map/pallas_call | solution.py:544
